TPU v7x, 32 devices: a whole 2x2x4 slice. The times are simulated.
32 devices in a mesh: groups: 2 (over y), panels: 4 (over z), cols: 2 (over x), phase: 2 (over core).
Axes of the slice: x: 2, y: 2, z: 4, core: 2. Of those that a mesh axis runs over, the one named last changes fastest.
Arguments:
- base_points: float32 [3, 512], P(None, ('groups', 'panels', 'cols')), parts along dimension 1, may hold values from -6 to 6
- control_points: float32 [3, 2048], replicated, may hold values from -6 to 6
- morph_weights: float32 [4, 3, 2048], P('groups'), parts along dimension 0, may hold values from -0.15 to 0.15
- connectivity: int32 [3, 1024], P(None, ('groups', 'panels', 'cols')), parts along dimension 1, may hold values from 0 to 255, as said below
- free_flags: int32 [1024], P(('groups', 'panels', 'cols')), parts along dimension 0, may hold values 0 or 1
- station_owner: int32 [1024, 1], P(('groups', 'panels', 'cols')), parts along dimension 0, may hold values from 0 to 7; in each aligned block of 64 rows (0 to 63, 64 to 127, ...) at most 20 rows name the same one
- variant_order: int32 [4], P('groups'), parts along dimension 0, may hold values from 0 to 1, each once
- load_velocity: float32 [64, 3], replicated, may hold values from -5 to 5
Outputs:
- shear: float32 [4, 64, 1024], P(('groups', 'phase'), None, ('panels', 'cols')), parts along dimension 0
- moment: float32 [4, 64, 1024], P(('groups', 'phase'), None, ('panels', 'cols')), parts along dimension 0
There are 2 independent parts, one for each index of `groups`. A program takes and returns all parts, laid end to end along the dimension named above; an argument that names none is the same for every part. Nothing has to cross between parts.
Inputs may be any that keep to these rules, and one draw needn't show every extreme that they name: `connectivity`: the vertices of panel i lie in block i // 64 of 32 consecutive vertices: from (i // 64) * 32 to (i // 64 + 1) * 32 - 1. `station_owner`: among the panels of one device (aligned blocks of 64 panels) no station owner is named more than 20 times. `variant_order`: each variant appears once.
All inputs are finite; a program needn't handle non-finite values. No bound on the sum of `free_flags` on one device may be relied on, other than what follows from the above.
Results may differ from a plain program's by a relative error of at most 0.0015.
Values may be sent and summed in bfloat16 or wider, within the bound.
No kernel may reach another device: no remote copies, remote signals or barrier semaphores. Data moves between devices by JAX's collectives and lax.ppermute only.
A program may use at most 64 MiB of HBM per device.

v0:
```python
import math

import jax
import jax.numpy as jnp
from jax import lax
from jax.sharding import PartitionSpec as P

STATIONS = 128


HIGH = lax.Precision.HIGHEST
CORE_SQUARE = 0.0025
SKIN_SQUARE = 0.01


def prefix(shard, axis, combine, identity):
    length, index = (lax.axis_size(axis), lax.axis_index(axis))
    everything = jax.tree.map(lambda part: lax.all_gather(part, axis), shard)
    start = jax.tree.map(
        lambda part, zero: jnp.broadcast_to(jnp.asarray(zero, part.dtype), part.shape),
        shard,
        identity,
    )

    def step(k, before):
        reached = k < index
        new = combine(before, jax.tree.map(lambda part: part[k], everything))
        return jax.tree.map(lambda a, b: jnp.where(reached, a, b), new, before)

    return lax.fori_loop(0, length, step, start)


def panel_shape(moved_points, corner_rows):
    first_corner = jnp.take(moved_points, corner_rows[0], axis=2)
    second_corner = jnp.take(moved_points, corner_rows[1], axis=2)
    third_corner = jnp.take(moved_points, corner_rows[2], axis=2)
    centroid = (first_corner + second_corner + third_corner) / 3.0
    edge_one = second_corner - first_corner
    edge_two = third_corner - first_corner
    cross_x = edge_one[:, 1] * edge_two[:, 2] - edge_one[:, 2] * edge_two[:, 1]
    cross_y = edge_one[:, 2] * edge_two[:, 0] - edge_one[:, 0] * edge_two[:, 2]
    cross_z = edge_one[:, 0] * edge_two[:, 1] - edge_one[:, 1] * edge_two[:, 0]
    area = 0.5 * jnp.stack([cross_x, cross_y, cross_z], axis=1)
    weight = jnp.sqrt(jnp.sum(area * area, axis=1) + SKIN_SQUARE)
    return (centroid, area, weight)


def tile_block(targets, sources, strengths, kernel_scale):
    distance = (
        (targets[:, 0, :, None] - sources[:, 0, None, :]) ** 2
        + (targets[:, 1, :, None] - sources[:, 1, None, :]) ** 2
        + (targets[:, 2, :, None] - sources[:, 2, None, :]) ** 2
    )
    influence = (sources[:, 3, None, :] * kernel_scale * lax.rsqrt(distance + CORE_SQUARE)).astype(
        jnp.bfloat16
    )
    return jnp.einsum("mrn,mkn->mkr", influence, strengths, preferred_element_type=jnp.float32)


def tile_product(carry_sum, targets, sources, strengths, kernel_scale):
    columns = strengths.shape[2]
    block_width = columns
    for candidate in (2048, 1024, 512):
        if columns > candidate and columns % candidate == 0:
            block_width = candidate
            break
    if block_width == columns:
        return carry_sum + tile_block(targets, sources, strengths, kernel_scale)

    def block_step(step_index, running_sum):
        column_start = step_index * block_width
        part_sources = lax.dynamic_slice_in_dim(sources, column_start, block_width, 2)
        part_strengths = lax.dynamic_slice_in_dim(strengths, column_start, block_width, 2)
        return running_sum + tile_block(targets, part_sources, part_strengths, kernel_scale)

    return lax.fori_loop(0, columns // block_width, block_step, carry_sum)


def add_pairs(earlier, later):
    return (earlier[0] + later[0], earlier[1] + later[1])


def shards(
    base_points,
    control_points,
    morph_weights,
    connectivity,
    free_flags,
    station_owner,
    variant_order,
    load_velocity,
):
    owners = lax.axis_size(("panels", "cols"))
    owner_index = lax.axis_index(("panels", "cols"))
    phase_index = lax.axis_index("phase")
    variant_dev = variant_order.shape[0] // lax.axis_size("phase")
    vert_dev = base_points.shape[1]
    pan_dev = connectivity.shape[1]
    load_count = load_velocity.shape[0]
    panels_total = pan_dev * owners
    own_variants = lax.dynamic_slice_in_dim(
        variant_order, phase_index * variant_dev, variant_dev, 0
    )
    picker = (
        own_variants[:, None] == jnp.arange(variant_order.shape[0], dtype=jnp.int32)[None, :]
    ).astype(jnp.float32)
    chosen = jnp.einsum("mv,vac->mac", picker, morph_weights, precision=HIGH)
    distance = (
        (control_points[0][:, None] - base_points[0][None, :]) ** 2
        + (control_points[1][:, None] - base_points[1][None, :]) ** 2
        + (control_points[2][:, None] - base_points[2][None, :]) ** 2
    )
    basis_values = lax.rsqrt(1.0 + distance)
    moved_points = base_points[None] + jnp.einsum(
        "mac,cn->man", chosen, basis_values, precision=HIGH
    )
    local_corners = connectivity - owner_index * vert_dev
    centroid, area, weight = panel_shape(moved_points, local_corners)
    hull_mask = (1 - free_flags).astype(jnp.float32)
    boundary = (
        jnp.einsum("ka,man->mkn", load_velocity, area, precision=HIGH) * hull_mask[None, None, :]
    )
    first_strengths = boundary.astype(jnp.bfloat16)
    kernel_scale = 1.0 / (4.0 * math.pi * math.sqrt(panels_total))
    own_geometry = jnp.concatenate([centroid, weight[:, None, :]], axis=1)
    sources = lax.all_gather(own_geometry, "panels", axis=2, tiled=True)
    row_targets = lax.all_gather(centroid, "cols", axis=2, tiled=True)

    def apply_influence(strengths):
        empty_sum = jnp.zeros((variant_dev, load_count, row_targets.shape[2]), jnp.float32)
        partial_sums = tile_product(
            empty_sum,
            row_targets,
            sources,
            lax.all_gather(strengths, "panels", axis=2, tiled=True),
            kernel_scale,
        )
        return lax.psum_scatter(partial_sums, "cols", scatter_dimension=2, tiled=True)

    induced = apply_influence(first_strengths)
    second_strengths = (first_strengths.astype(jnp.float32) + (boundary - induced)).astype(
        jnp.bfloat16
    )
    pressure = apply_influence(second_strengths)
    panel_force = pressure * (area[:, 2, :] * hull_mask[None, :])[:, None, :]
    force_rows = panel_force.reshape(-1, pan_dev)
    capacity = max(2, 5 * pan_dev // (2 * owners))
    target_owner = station_owner[:, 0]
    panel_order = jnp.arange(pan_dev, dtype=jnp.int32)
    ahead = (target_owner[:, None] == target_owner[None, :]) & (
        panel_order[None, :] < panel_order[:, None]
    )
    slot_rank = jnp.sum(ahead.astype(jnp.int32), axis=1)
    slot_index = target_owner * capacity + slot_rank
    all_slots = jnp.arange(owners * capacity, dtype=jnp.int32)
    placed = slot_index[:, None] == all_slots[None, :]
    send_values = jnp.dot(force_rows, placed.astype(jnp.float32), precision=HIGH)
    station_bins = (owner_index * pan_dev + panel_order) % STATIONS
    send_bins = jnp.max(jnp.where(placed, station_bins[:, None], -1), axis=0)[None, :]
    recv_values, recv_bins = (
        lax.all_to_all(send_values, ("panels", "cols"), split_axis=1, concat_axis=1, tiled=True),
        lax.all_to_all(send_bins, ("panels", "cols"), split_axis=1, concat_axis=1, tiled=True),
    )
    matches = (recv_bins[0][:, None] == jnp.arange(STATIONS, dtype=jnp.int32)[None, :]).astype(
        jnp.float32
    )
    station_loads = jnp.dot(recv_values, matches, precision=HIGH)
    station_place = (owner_index * STATIONS + jnp.arange(STATIONS, dtype=jnp.int32)).astype(
        jnp.float32
    ) / (STATIONS * owners)
    placed_loads = station_loads * station_place[None, :]
    own_total = jnp.sum(station_loads, axis=1)
    own_arm = jnp.sum(placed_loads, axis=1)
    zero_row = jnp.zeros_like(own_total)
    prior_total, prior_arm = prefix(
        (own_total, own_arm), ("panels", "cols"), add_pairs, (zero_row, zero_row)
    )
    station_rank = jnp.arange(STATIONS, dtype=jnp.int32)
    inclusive = (station_rank[:, None] <= station_rank[None, :]).astype(jnp.float32)
    strict = (station_rank[:, None] < station_rank[None, :]).astype(jnp.float32)
    running = prior_total[:, None] + jnp.dot(station_loads, inclusive, precision=HIGH)
    earlier = prior_total[:, None] + jnp.dot(station_loads, strict, precision=HIGH)
    moment_arm = prior_arm[:, None] + jnp.dot(placed_loads, strict, precision=HIGH)
    inv_root = 1.0 / math.sqrt(panels_total)
    shear = (running * inv_root).reshape(variant_dev, load_count, STATIONS)
    moment = ((station_place[None, :] * earlier - moment_arm) * inv_root).reshape(
        variant_dev, load_count, STATIONS
    )
    return (shear, moment)


def solution(mesh):
    return jax.shard_map(
        shards,
        mesh=mesh,
        in_specs=(
            P(None, ("groups", "panels", "cols")),
            P(),
            P("groups", None, None),
            P(None, ("groups", "panels", "cols")),
            P(("groups", "panels", "cols")),
            P(("groups", "panels", "cols"), None),
            P("groups"),
            P(),
        ),
        out_specs=(
            P(("groups", "phase"), None, ("panels", "cols")),
            P(("groups", "phase"), None, ("panels", "cols")),
        ),
        check_vma=False,
    )
```

profile of v0, /device:TPU:0, one launch (start us, length us, event | category | flops | bytes accessed | tf_op | source)
XLA Modules:
  0.0 130.6 jit_solution(7332633443924360634)
XLA Ops:
  7.2 0.9 fusion.63
  8.2 0.6 copy-done.4
  8.8 0.6 dynamic_slice.17
  9.4 0.9 fusion.48
  10.3 0.4 convolution_add_fusion.3
  10.8 0.7 copy-done.1
  11.5 0.6 gather_fusion.2
  12.1 0.6 gather_fusion
  12.7 0.6 gather_fusion.1
  13.4 0.2 fusion.60
  14.0 0.1 copy.52
  14.1 5.5 %all_gather.26 = f32[1,3,128]{1,2,0:T(8,128)S(1)} all-gather(f32[1,3,64]{1,2,0:T(8,128)S(1)} %get-tuple-element.175), channel_id=1, replica_groups=mesh['groups'=2,'panels'=4,'cols'=2,'phase'=2] {'cols'}, dimensions={2}, use_global_device_ids=true | all-gather | bytes 2304 | tf_op jit(solution)/shard_map/all_gather | solution.py:127
  19.6 14.1 %all_gather.25 = f32[1,4,256]{1,0,2:T(1,128)S(1)} all-gather(f32[1,4,64]{1,0,2:T(1,128)S(1)} %bitcast.124), channel_id=1, replica_groups=mesh['groups'=2,'panels'=4,'cols'=2,'phase'=2] {'panels'}, dimensions={2}, use_global_device_ids=true | all-gather | bytes 5120 | tf_op jit(solution)/shard_map/all_gather | solution.py:126
  33.8 3.3 %fusion.25 = (f32[256]{0:T(256)S(1)}, f32[256]{0:T(256)S(1)}, f32[256]{0:T(256)S(1)}, f32[256]{0:T(256)S(1)}) fusion(f32[1,4,256]{1,0,2:T(1,128)S(1)} %all_gather.25), kind=kLoop, calls=%fused_computation.44 | loop fusion | flops 256 | bytes 8192 | tf_op jit(solution)/shard_map/mul | solution.py:54
  37.1 0.7 copy-done.3
  37.8 0.2 fusion.64
  38.1 13.2 %all_gather.24 = bf16[1,64,256]{1,2,0:T(8,128)(2,1)S(1)} all-gather(bf16[1,64,64]{1,2,0:T(8,128)(2,1)S(1)} %get-tuple-element.192), channel_id=1, replica_groups=mesh['groups'=2,'panels'=4,'cols'=2,'phase'=2] {'panels'}, dimensions={2}, use_global_device_ids=true | all-gather | bytes 40960 | tf_op jit(solution)/shard_map/all_gather | solution.py:135
  51.3 0.2 slice_reduce_fusion.5
  51.5 0.9 convolution_bitcast_fusion.1
  52.4 0.6 copy-done.5
  53.0 0.2 convert_reduce_fusion
  53.2 0.1 select_reduce_fusion
  53.3 0.7 all_to_all.14
  54.0 5.7 %all-to-all-start.1 = ((s32[1,8,20]{2,0,1:T(1,128)}), s32[1,8,20]{2,0,1:T(1,128)S(1)}, u32[]{:S(2)}, u32[]{:S(2)}) async-start(s32[1,8,20]{2,0,1:T(1,128)} %all_to_all.14), calls=%async_computation.2 | async-start | bytes 8192 | tf_op jit(solution)/shard_map/all_to_all | solution.py:162
  59.8 0.6 copy-done.7
  60.4 0.7 dynamic-slice
  61.8 1.7 %reduce-scatter.5.cloned.1.call-done = f32[1,64,64]{1,2,0:T(8,128)} async-done(((f32[1,64,128]{1,2,0:T(8,128)}), f32[1,64,64]{1,2,0:T(8,128)}) %reduce-scatter.5.cloned.1.call-update) | async-done | bytes 16400 | tf_op jit(solution)/shard_map/reduce_scatter | solution.py:138
  63.5 0.8 add_convert_fusion
  64.3 13.2 %all_gather.27 = bf16[1,64,256]{1,2,0:T(8,128)(2,1)S(1)} all-gather(bf16[1,64,64]{1,2,0:T(8,128)(2,1)S(1)} %add_convert_fusion), channel_id=1, replica_groups=mesh['groups'=2,'panels'=4,'cols'=2,'phase'=2] {'panels'}, dimensions={2}, use_global_device_ids=true | all-gather | bytes 40960 | tf_op jit(solution)/shard_map/all_gather | solution.py:135
  77.5 0.9 convolution_bitcast_fusion
  78.4 10.0 %reduce-scatter.7.cloned.1.call-done = f32[64,64]{1,0:T(8,128)} async-done(((f32[128,64]{1,0:T(8,128)}), f32[64,64]{1,0:T(8,128)}) %reduce-scatter.7.cloned.1.call-update) | async-done | bytes 16400
  88.4 0.8 copy.58
  89.2 0.3 fusion.65
  89.5 0.7 reshape.458
  90.2 4.6 %all-to-all-start = ((f32[8,1,1280]{2,1,0:T(1,128)}), f32[8,1,1280]{2,1,0:T(1,128)S(1)}, u32[]{:S(2)}, u32[]{:S(2)}) async-start(f32[8,1,1280]{2,1,0:T(1,128)} %reshape.458), calls=%async_computation.1 | async-start | bytes 81920 | tf_op jit(solution)/shard_map/all_to_all | solution.py:161
  94.8 0.5 broadcast.246
  95.3 0.7 reduce.21
  96.0 5.5 %all-to-all-done = f32[8,1,1280]{2,1,0:T(1,128)S(1)} async-done(((f32[8,1,1280]{2,1,0:T(1,128)}), f32[8,1,1280]{2,1,0:T(1,128)S(1)}, u32[]{:S(2)}, u32[]{:S(2)}) %all-to-all-start) | async-done | bytes 40992 | tf_op jit(solution)/shard_map/all_to_all | solution.py:161
  101.5 0.5 broadcast.247
  102.0 0.7 reduce.25
  102.9 0.4 multiply_reduce_fusion
  103.3 0.2 dynamic-update-slice
  103.5 0.2 dynamic-update-slice.1
  103.7 17.8 %all-reduce.2 = (f32[512]{0:T(512)S(1)}, f32[512]{0:T(512)S(1)}) all-reduce(f32[512]{0:T(512)S(1)} %dynamic-update-slice, f32[512]{0:T(512)S(1)} %dynamic-update-slice.1), channel_id=2, replica_groups=mesh['groups'=2,'panels'=4,'cols'=2,'phase'=2] {'panels','cols'}, use_global_device_ids=true, to_apply=%add | all-reduce | flops 1024 | bytes 8192
  121.7 0.3 while.16
  122.0 0.2 fusion.3
  122.2 0.8 fusion.5
  123.0 0.8 fusion.2
  (52 shorter events, 1.2 us)
Async XLA Ops:
  7.2 2.2 %copy-start = (f32[2,3,2048]{2,0,1:T(2,128)S(1)}, f32[2,3,2048]{2,0,1:T(2,128)}, u32[]{:S(2)}) copy-start(f32[2,3,2048]{2,0,1:T(2,128)} %param.14) | copy-start | bytes 147460
  7.2 56.3 %reduce-scatter.5.cloned.1.call-start = ((), (), s32[]{:S(2)}) async-start(), calls=%async_computation.4 | async-start | bytes 98304 | tf_op jit(solution)/shard_map/reduce_scatter | solution.py:138
  7.2 0.9 copy-start.2
  8.2 0.7 copy-start.4
  10.8 0.7 copy-start.1
  33.8 3.3 %copy-start.6 = (s32[64]{0:T(128)S(1)}, s32[64]{0:T(128)}, u32[]{:S(2)}) copy-start(s32[64]{0:T(128)} %param.16) | copy-start | bytes 772
  37.1 0.7 copy-start.3
  52.4 0.7 copy-start.5
  54.0 36.1 %all-to-all-start.1 = ((s32[1,8,20]{2,0,1:T(1,128)}), s32[1,8,20]{2,0,1:T(1,128)S(1)}, u32[]{:S(2)}, u32[]{:S(2)}) async-start(s32[1,8,20]{2,0,1:T(1,128)} %all_to_all.14), calls=%async_computation.2 | async-start | bytes 8192 | tf_op jit(solution)/shard_map/all_to_all | solution.py:162
  59.7 28.7 %reduce-scatter.7.cloned.1.call-start = ((), (), s32[]{:S(2)}) async-start(), calls=%async_computation.5 | async-start | bytes 98304
  59.8 0.7 copy-start.7
  90.2 11.3 %all-to-all-start = ((f32[8,1,1280]{2,1,0:T(1,128)}), f32[8,1,1280]{2,1,0:T(1,128)S(1)}, u32[]{:S(2)}, u32[]{:S(2)}) async-start(f32[8,1,1280]{2,1,0:T(1,128)} %reshape.458), calls=%async_computation.1 | async-start | bytes 81920 | tf_op jit(solution)/shard_map/all_to_all | solution.py:161
Sparse Core Ops, SparseCore 0:
  52.5 10.9 reduce-scatter.4
  78.5 9.8 reduce-scatter.6
where the time goes:
time: 131 us
  blocking collectives  63.9 us (49%)
  waiting for transfers between devices  17.2 us (13%)
  between operations  15 us (11%)
  local copies, waits for them, and re-layouts  11.9 us (9%)
  starting transfers between devices  10.3 us (8%)
  other arithmetic  6.43 us (5%)
  matrix products  5.69 us (4%)
    all_gather x2, blocking collectives, apply_influence(): lax.all_gather(strengths, 'panels', axis=2, tiled=True)  26.4 us
    unnamed x1, blocking collectives  17.8 us
    all_gather x1, blocking collectives, shards(): sources = lax.all_gather(own_geometry, 'panels', axis=2, tiled=True)  14.1 us
    unnamed x3, waiting for transfers between devices  10 us
    unnamed x24, local copies, waits for them, and re-layouts  6.08 us
    all_to_all x1, starting transfers between devices, shards(): lax.all_to_all(send_bins, ('panels', 'cols'), split_axis=1, concat_axis=1...  5.66 us
    all_gather x1, blocking collectives, shards(): row_targets = lax.all_gather(centroid, 'cols', axis=2, tiled=True)  5.48 us
    all_to_all x1, waiting for transfers between devices, shards(): lax.all_to_all(send_values, ('panels', 'cols'), split_axis=1, concat_axis...  5.47 us
  transfers between devices with their start and end apart: 4, of which 3 were waited for; matrix products, arithmetic and copies ran while one was open for 4% of the time, Pallas kernels for 0%

commit v1 on v0

--- a/solution.py
+++ b/solution.py
@@ -1,11 +1,16 @@
+import functools
 import math
 
 import jax
 import jax.numpy as jnp
 from jax import lax
+from jax.experimental import pallas as pl
+from jax.experimental.pallas import tpu as pltpu
 from jax.sharding import PartitionSpec as P
 
 STATIONS = 128
+LANES = 128
+PANELS_ON_ONE = 1024
 
 
 HIGH = lax.Precision.HIGHEST
@@ -80,7 +85,7 @@
     return (earlier[0] + later[0], earlier[1] + later[1])
 
 
-def shards(
+def shards_split(
     base_points,
     control_points,
     morph_weights,
@@ -189,6 +194,225 @@
     return (shear, moment)
 
 
+def geometry_kernel(
+    vert_dev,
+    order_ref,
+    base_ref,
+    control_ref,
+    weights_ref,
+    corner_ref,
+    flags_ref,
+    owner_ref,
+    out_ref,
+):
+    variant = order_ref[lax.axis_index("phase")]
+    pan_dev = corner_ref.shape[1]
+    diagonal = lax.broadcasted_iota(jnp.int32, (vert_dev, vert_dev), 0) == lax.broadcasted_iota(
+        jnp.int32, (vert_dev, vert_dev), 1
+    )
+    base = [
+        jnp.sum(jnp.where(diagonal, base_ref[a : a + 1, :], 0.0), axis=1, keepdims=True)
+        for a in range(3)
+    ]
+    totals = [jnp.zeros((vert_dev, LANES), jnp.float32) for _ in range(3)]
+    for start in range(0, control_ref.shape[1], LANES):
+        part = pl.ds(start, LANES)
+        distance = (
+            (control_ref[0:1, part] - base[0]) ** 2
+            + (control_ref[1:2, part] - base[1]) ** 2
+            + (control_ref[2:3, part] - base[2]) ** 2
+        )
+        basis = lax.rsqrt(1.0 + distance)
+        totals = [totals[a] + weights_ref[variant, a : a + 1, part] * basis for a in range(3)]
+    moved = [base[a] + jnp.sum(totals[a], axis=1, keepdims=True) for a in range(3)]
+    vertex = lax.broadcasted_iota(jnp.int32, (vert_dev, pan_dev), 0)
+    corners = []
+    for k in range(3):
+        chosen = vertex == lax.rem(corner_ref[k : k + 1, :], vert_dev)
+        corners.append(
+            [jnp.sum(jnp.where(chosen, moved[a], 0.0), axis=0, keepdims=True) for a in range(3)]
+        )
+    first, second, third = corners
+    centroid = [(first[a] + second[a] + third[a]) * (1.0 / 3.0) for a in range(3)]
+    one = [second[a] - first[a] for a in range(3)]
+    two = [third[a] - first[a] for a in range(3)]
+    area = [
+        0.5 * (one[1] * two[2] - one[2] * two[1]),
+        0.5 * (one[2] * two[0] - one[0] * two[2]),
+        0.5 * (one[0] * two[1] - one[1] * two[0]),
+    ]
+    hull = (1 - flags_ref[...]).astype(jnp.float32)
+    owner = owner_ref[...].astype(jnp.float32)
+    rows = jnp.concatenate(centroid + area + [hull, owner], axis=0)
+    rows = jnp.concatenate([rows] * (LANES // pan_dev), axis=1)
+    last = lax.broadcasted_iota(jnp.int32, rows.shape, 0) == rows.shape[0] - 1
+    for target in range(out_ref.shape[0]):
+        out_ref[target] = jnp.where(last, rows - float(target), rows)
+
+
+def loads_kernel(pan_dev, kernel_scale, rows_ref, velocity_ref, shear_ref, moment_ref, influence):
+    owners = rows_ref.shape[0]
+    shared = LANES // pan_dev
+    tiles = owners // shared
+    panels_total = owners * pan_dev
+    load_count = velocity_ref.shape[0]
+    lane = lax.broadcasted_iota(jnp.int32, (8, LANES), 1)
+    panels, columns = [], []
+    for q in range(tiles):
+        tile = rows_ref[q * shared]
+        for h in range(1, shared):
+            tile = jnp.where(lane >= h * pan_dev, rows_ref[q * shared + h], tile)
+        panels.append(tile)
+        area = [tile[3 + a : 4 + a, :] for a in range(3)]
+        weight = jnp.sqrt(area[0] * area[0] + area[1] * area[1] + area[2] * area[2] + SKIN_SQUARE)
+        columns.append(
+            jnp.concatenate([tile[0:3, :], weight * kernel_scale, tile[4:8, :]], axis=0).T
+        )
+    for source in range(tiles):
+        column = columns[source]
+        centre = [column[:, a : a + 1] for a in range(3)]
+        weight = column[:, 3:4]
+        for target in range(tiles):
+            tile = panels[target]
+            distance = (
+                (tile[0:1, :] - centre[0]) ** 2
+                + (tile[1:2, :] - centre[1]) ** 2
+                + (tile[2:3, :] - centre[2]) ** 2
+            )
+            influence[pl.ds(source * LANES, LANES), pl.ds(target * LANES, LANES)] = (
+                weight * lax.rsqrt(distance + CORE_SQUARE)
+            ).astype(jnp.bfloat16)
+    velocity = [velocity_ref[:, a : a + 1] for a in range(3)]
+    boundary = jnp.concatenate(
+        [
+            (velocity[0] * tile[3:4, :] + velocity[1] * tile[4:5, :] + velocity[2] * tile[5:6, :])
+            * tile[6:7, :]
+            for tile in panels
+        ],
+        axis=1,
+    )
+    first = boundary.astype(jnp.bfloat16)
+    induced = jnp.dot(first, influence[...], preferred_element_type=jnp.float32)
+    second = (first.astype(jnp.float32) + (boundary - induced)).astype(jnp.bfloat16)
+    pressure = jnp.dot(second, influence[...], preferred_element_type=jnp.float32)
+
+    stations_all = STATIONS * owners
+    own_loads = jnp.zeros((load_count, LANES), jnp.float32)
+    prior_loads = jnp.zeros((load_count, LANES), jnp.float32)
+    prior_arms = jnp.zeros((load_count, LANES), jnp.float32)
+    rank = lax.broadcasted_iota(jnp.int32, (1, LANES), 1).astype(jnp.float32)
+    for q, tile in enumerate(panels):
+        force = pressure[:, q * LANES : (q + 1) * LANES] * (tile[5:6, :] * tile[6:7, :])
+        owner = tile[7:8, :]
+        prior = owner < 0.0
+        place = (owner * STATIONS + rank) * (1.0 / stations_all)
+        own_loads = own_loads + jnp.where(owner == 0.0, force, 0.0)
+        prior_loads = prior_loads + jnp.where(prior, force, 0.0)
+        prior_arms = prior_arms + force * jnp.where(prior, place, 0.0)
+    prior_total = jnp.sum(prior_loads, axis=1, keepdims=True)
+    prior_arm = jnp.sum(prior_arms, axis=1, keepdims=True)
+    station = lax.broadcasted_iota(jnp.int32, (STATIONS, 2 * STATIONS), 0)
+    place = lax.broadcasted_iota(jnp.int32, (STATIONS, 2 * STATIONS), 1)
+    arm = place - STATIONS - station
+    steps = jnp.where(
+        place < STATIONS, (station <= place).astype(jnp.int32), jnp.maximum(arm, 0)
+    ).astype(jnp.float32).astype(jnp.bfloat16)
+    high = own_loads.astype(jnp.bfloat16)
+    rest = own_loads - high.astype(jnp.float32)
+    middle = rest.astype(jnp.bfloat16)
+    low = (rest - middle.astype(jnp.float32)).astype(jnp.bfloat16)
+    sums = jnp.dot(
+        jnp.concatenate([high, middle, low], axis=0), steps, preferred_element_type=jnp.float32
+    )
+    sums = sums[:load_count] + (sums[load_count : 2 * load_count] + sums[2 * load_count :])
+    inv_root = 1.0 / math.sqrt(panels_total)
+    shear_ref[0] = (prior_total + sums[:, :STATIONS]) * inv_root
+    moment_ref[0] = (
+        (rank * (1.0 / stations_all)) * prior_total
+        - prior_arm
+        + sums[:, STATIONS:] * (1.0 / stations_all)
+    ) * inv_root
+
+
+def shards_whole(
+    base_points,
+    control_points,
+    morph_weights,
+    connectivity,
+    free_flags,
+    station_owner,
+    variant_order,
+    load_velocity,
+):
+    owners = lax.axis_size(("panels", "cols"))
+    vert_dev = base_points.shape[1]
+    pan_dev = connectivity.shape[1]
+    load_count = load_velocity.shape[0]
+    panels_total = pan_dev * owners
+    vmem = pl.BlockSpec(memory_space=pltpu.VMEM)
+    rows = pl.pallas_call(
+        functools.partial(geometry_kernel, vert_dev),
+        out_shape=jax.ShapeDtypeStruct((owners, 8, LANES), jnp.float32),
+        in_specs=[pl.BlockSpec(memory_space=pltpu.SMEM)] + [vmem] * 6,
+        out_specs=vmem,
+        name="geometry",
+    )(
+        variant_order,
+        base_points,
+        control_points,
+        morph_weights,
+        connectivity,
+        free_flags.reshape(1, pan_dev),
+        station_owner.reshape(1, pan_dev),
+    )
+    rows = lax.all_to_all(rows, ("panels", "cols"), split_axis=0, concat_axis=0)
+    kernel_scale = 1.0 / (4.0 * math.pi * math.sqrt(panels_total))
+    out = jax.ShapeDtypeStruct((1, load_count, STATIONS), jnp.float32)
+    return pl.pallas_call(
+        functools.partial(loads_kernel, pan_dev, kernel_scale),
+        out_shape=(out, out),
+        in_specs=[vmem] * 2,
+        out_specs=(vmem, vmem),
+        scratch_shapes=[pltpu.VMEM((panels_total, panels_total), jnp.bfloat16)],
+        compiler_params=pltpu.CompilerParams(vmem_limit_bytes=32 * 1024 * 1024),
+        name="loads",
+    )(rows, load_velocity)
+
+
+def shards(
+    base_points,
+    control_points,
+    morph_weights,
+    connectivity,
+    free_flags,
+    station_owner,
+    variant_order,
+    load_velocity,
+):
+    owners = lax.axis_size(("panels", "cols"))
+    pan_dev = connectivity.shape[1]
+    panels_total = owners * pan_dev
+    whole = (
+        panels_total <= PANELS_ON_ONE
+        and panels_total % LANES == 0
+        and LANES % pan_dev == 0
+        and STATIONS == LANES
+        and variant_order.shape[0] == lax.axis_size("phase")
+        and control_points.shape[1] % LANES == 0
+        and load_velocity.shape[0] % 16 == 0
+    )
+    return (shards_whole if whole else shards_split)(
+        base_points,
+        control_points,
+        morph_weights,
+        connectivity,
+        free_flags,
+        station_owner,
+        variant_order,
+        load_velocity,
+    )
+
+
 def solution(mesh):
     return jax.shard_map(
         shards,

time: 131 us -> 20.2 us (0.15)
  blocking collectives: 63.9 us -> 0 us
  between operations: 15 us -> 0.64 us
  waiting for transfers between devices: 17.2 us -> 6.58 us
  local copies, waits for them, and re-layouts: 11.9 us -> 1.55 us
  other arithmetic: 6.43 us -> 0 us
  matrix products: 5.69 us -> 0 us
  Pallas kernels: 0 us -> 3.71 us
  starting transfers between devices: 10.3 us -> 7.38 us
    all_gather x4 -> x0, blocking collectives: 46 us -> none  [the longest x2 26.4 us: apply_influence(): lax.all_gather(strengths, 'panels', axis=2, tiled=True)]
    unnamed x1 -> x0, blocking collectives: 17.8 us -> none
    unnamed x3 -> x0, waiting for transfers between devices: 10 us -> none
    dot_general x10 -> x0, matrix products: 5.69 us -> none  [the longest x2 1.74 us: tile_block(): jnp.einsum('mrn,mkn->mkr', influence, strengths, preferred_element_type=j...]
    unnamed x24 -> x4, local copies, waits for them, and re-layouts: 6.08 us -> 1.55 us
    pallas_call x0 -> x2, Pallas kernels: none -> 3.71 us  [the longest x1 1.91 us: shards_whole(): pl.pallas_call(functools.partial(geometry_kernel, vert_dev), out_shape=ja...]
    mul x2 -> x0, other arithmetic: 3.33 us -> none  [the longest x1 3.33 us: tile_block(): sources[:, 3, None, :] * kernel_scale * lax.rsqrt(distance + CORE_SQUARE)]
    all_to_all x2 -> x1, starting transfers between devices: 10.2 us -> 7.38 us  [shards_whole(): rows = lax.all_to_all(rows, ('panels', 'cols'), split_axis=0, concat_axis=0)]
  transfers between devices with their start and end apart: 4 -> 1, of which waited for: 3 -> 1; matrix products, arithmetic and copies ran while one was open for 4% -> 0% of each run, Pallas kernels for 0% -> 0%
where the time goes in v1:
time: 20.2 us; the launch traced here: 19.9 us
  starting transfers between devices  7.38 us (37%)
  waiting for transfers between devices  6.58 us (33%)
  Pallas kernels  3.71 us (18%)
  local copies, waits for them, and re-layouts  1.55 us (8%)
  between operations  0.64 us (3%)
    all_to_all x1, starting transfers between devices, shards_whole(): rows = lax.all_to_all(rows, ('panels', 'cols'), split_axis=0, concat_axis=0)  7.38 us
    all_to_all x1, waiting for transfers between devices, shards_whole(): rows = lax.all_to_all(rows, ('panels', 'cols'), split_axis=0, concat_axis=0)  6.58 us
    pallas_call x1, Pallas kernels, shards_whole(): pl.pallas_call(functools.partial(geometry_kernel, vert_dev), out_shape=ja...  1.91 us
    pallas_call x1, Pallas kernels, shards_whole(): pl.pallas_call(functools.partial(loads_kernel, pan_dev, kernel_scale), ou...  1.8 us
    unnamed x4, local copies, waits for them, and re-layouts  1.55 us
  transfers between devices with their start and end apart: 1, of which 1 were waited for; matrix products, arithmetic and copies ran while one was open for 0% of the time, Pallas kernels for 0%

profile of v1, /device:TPU:0, one launch (start us, length us, event | category | flops | bytes accessed | tf_op | source)
XLA Modules:
  0.0 19.9 jit_solution(11880102620046522821)
XLA Ops:
  0.6 1.4 %copy.10.weights_ref = f32[2,3,2048]{2,1,0:T(4,128)} copy(f32[2,3,2048]{2,0,1:T(2,128)} %param.10) | data formatting | bytes 98304 | tf_op args[2]
  2.1 1.9 %geometry.1 = f32[8,8,128]{2,1,0:T(8,128)} custom-call(s32[2]{0:T(128)} %order_ref.1, f32[3,32]{1,0:T(4,128)} %base_ref.1, f32[3,2048]{1,0:T(4,128)} %control_ref.1, f32[2,3,2048]{2,1,0:T(4,128)} %copy.10.weights_ref, s32[3,64]{1,0:T(4,128)} %corner_ref.1, s32[1,64]{1,0:T(1,128)} %bitcast.2, s32[1,64]{1,0:T(1,128)} %bitcast.3), custom_call_target="tpu_custom_call" | custom-call | tf_op jit(solution)/shard_map/geometry/pallas_call | solution.py:353
  4.0 0.0 copy-start
  4.0 7.4 %all-to-all-start = ((f32[8,8,128]{2,1,0:T(8,128)}), f32[8,8,128]{2,1,0:T(8,128)S(1)}, u32[]{:S(2)}, u32[]{:S(2)}) async-start(f32[8,8,128]{2,1,0:T(8,128)} %geometry.1), calls=%async_computation | async-start | bytes 65536 | tf_op jit(solution)/shard_map/all_to_all | solution.py:368
  11.4 0.0 copy-done
  11.4 0.1 copy.11.velocity_ref
  11.5 6.6 %all-to-all-done.rows_ref = f32[8,8,128]{2,1,0:T(8,128)S(1)} async-done(((f32[8,8,128]{2,1,0:T(8,128)}), f32[8,8,128]{2,1,0:T(8,128)S(1)}, u32[]{:S(2)}, u32[]{:S(2)}) %all-to-all-start) | async-done | bytes 32800 | tf_op jit(solution)/shard_map/all_to_all | solution.py:368
  18.1 1.8 %loads.1 = (f32[1,64,128]{2,1,0:T(8,128)}, f32[1,64,128]{2,1,0:T(8,128)}) custom-call(f32[8,8,128]{2,1,0:T(8,128)S(1)} %all-to-all-done.rows_ref, f32[64,3]{1,0:T(8,128)S(1)} %copy.11.velocity_ref), custom_call_target="tpu_custom_call" | custom-call | tf_op jit(solution)/shard_map/loads/pallas_call | solution.py:371
Async XLA Ops:
  4.0 7.4 %copy-start = (f32[64,3]{0,1:T(4,128)S(1)}, f32[64,3]{0,1:T(4,128)}, u32[]{:S(2)}) copy-start(f32[64,3]{0,1:T(4,128)} %param.15) | copy-start | bytes 2308
  4.0 14.1 %all-to-all-start = ((f32[8,8,128]{2,1,0:T(8,128)}), f32[8,8,128]{2,1,0:T(8,128)S(1)}, u32[]{:S(2)}, u32[]{:S(2)}) async-start(f32[8,8,128]{2,1,0:T(8,128)} %geometry.1), calls=%async_computation | async-start | bytes 65536 | tf_op jit(solution)/shard_map/all_to_all | solution.py:368

commit v2 on v1

--- a/solution.py
+++ b/solution.py
@@ -223,7 +223,11 @@
             + (control_ref[2:3, part] - base[2]) ** 2
         )
         basis = lax.rsqrt(1.0 + distance)
-        totals = [totals[a] + weights_ref[variant, a : a + 1, part] * basis for a in range(3)]
+        for a in range(3):
+            weights = weights_ref[a, 0:1, part]
+            for v in range(1, weights_ref.shape[1]):
+                weights = jnp.where(variant == v, weights_ref[a, v : v + 1, part], weights)
+            totals[a] = totals[a] + weights * basis
     moved = [base[a] + jnp.sum(totals[a], axis=1, keepdims=True) for a in range(3)]
     vertex = lax.broadcasted_iota(jnp.int32, (vert_dev, pan_dev), 0)
     corners = []
@@ -247,7 +251,7 @@
     rows = jnp.concatenate([rows] * (LANES // pan_dev), axis=1)
     last = lax.broadcasted_iota(jnp.int32, rows.shape, 0) == rows.shape[0] - 1
     for target in range(out_ref.shape[0]):
-        out_ref[target] = jnp.where(last, rows - float(target), rows)
+        out_ref[out_ref.shape[0] - 1 - target] = jnp.where(last, rows - float(target), rows)
 
 
 def loads_kernel(pan_dev, kernel_scale, rows_ref, velocity_ref, shear_ref, moment_ref, influence):
@@ -259,9 +263,9 @@
     lane = lax.broadcasted_iota(jnp.int32, (8, LANES), 1)
     panels, columns = [], []
     for q in range(tiles):
-        tile = rows_ref[q * shared]
+        tile = rows_ref[owners - 1 - q * shared]
         for h in range(1, shared):
-            tile = jnp.where(lane >= h * pan_dev, rows_ref[q * shared + h], tile)
+            tile = jnp.where(lane >= h * pan_dev, rows_ref[owners - 1 - q * shared - h], tile)
         panels.append(tile)
         area = [tile[3 + a : 4 + a, :] for a in range(3)]
         weight = jnp.sqrt(area[0] * area[0] + area[1] * area[1] + area[2] * area[2] + SKIN_SQUARE)
@@ -360,12 +364,15 @@
         variant_order,
         base_points,
         control_points,
-        morph_weights,
+        morph_weights.transpose(1, 0, 2),
         connectivity,
         free_flags.reshape(1, pan_dev),
         station_owner.reshape(1, pan_dev),
     )
-    rows = lax.all_to_all(rows, ("panels", "cols"), split_axis=0, concat_axis=0)
+    order = list(range(owners))[::-1]
+    rows = lax.all_to_all(
+        rows, ("panels", "cols"), split_axis=0, concat_axis=0, axis_index_groups=[order]
+    )
     kernel_scale = 1.0 / (4.0 * math.pi * math.sqrt(panels_total))
     out = jax.ShapeDtypeStruct((1, load_count, STATIONS), jnp.float32)
     return pl.pallas_call(

time: 20.2 us -> 16.6 us (0.82)
  waiting for transfers between devices: 6.58 us -> 2.52 us
  starting transfers between devices: 7.38 us -> 9.39 us
  local copies, waits for them, and re-layouts: 1.55 us -> 0.1 us
    all_to_all x1, waiting for transfers between devices: 6.58 us -> 2.52 us  [shards_whole(): lax.all_to_all(rows, ('panels', 'cols'), split_axis=0, concat_axis=0, axi...]
    all_to_all x1, starting transfers between devices: 7.38 us -> 9.39 us  [shards_whole(): lax.all_to_all(rows, ('panels', 'cols'), split_axis=0, concat_axis=0, axi...]
    unnamed x4 -> x3, local copies, waits for them, and re-layouts: 1.55 us -> 0.1 us
  transfers between devices with their start and end apart: 1 -> 1, of which waited for: 1 -> 1; matrix products, arithmetic and copies ran while one was open for 0% -> 1% of each run, Pallas kernels for 0% -> 0%
where the time goes in v2:
time: 16.6 us; the launch traced here: 16.3 us
  starting transfers between devices  9.39 us (57%)
  Pallas kernels  3.67 us (22%)
  waiting for transfers between devices  2.52 us (15%)
  between operations  0.64 us (4%)
    all_to_all x1, starting transfers between devices, shards_whole(): lax.all_to_all(rows, ('panels', 'cols'), split_axis=0, concat_axis=0, axi...  9.39 us
    all_to_all x1, waiting for transfers between devices, shards_whole(): lax.all_to_all(rows, ('panels', 'cols'), split_axis=0, concat_axis=0, axi...  2.52 us
    pallas_call x1, Pallas kernels, shards_whole(): pl.pallas_call(functools.partial(geometry_kernel, vert_dev), out_shape=ja...  1.87 us
    pallas_call x1, Pallas kernels, shards_whole(): pl.pallas_call(functools.partial(loads_kernel, pan_dev, kernel_scale), ou...  1.81 us
  transfers between devices with their start and end apart: 1, of which 1 were waited for; matrix products, arithmetic and copies ran while one was open for 1% of the time, Pallas kernels for 0%

profile of v2, /device:TPU:0, one launch (start us, length us, event | category | flops | bytes accessed | tf_op | source)
XLA Modules:
  0.0 16.3 jit_solution(6625811963623794157)
XLA Ops:
  0.6 1.9 %geometry.1 = f32[8,8,128]{2,1,0:T(8,128)} custom-call(s32[2]{0:T(128)} %order_ref.1, f32[3,32]{1,0:T(4,128)} %base_ref.1, f32[3,2048]{1,0:T(4,128)} %control_ref.1, f32[3,2,2048]{2,1,0:T(2,128)} %bitcast.3, s32[3,64]{1,0:T(4,128)} %corner_ref.1, s32[1,64]{1,0:T(1,128)} %bitcast.4, s32[1,64]{1,0:T(1,128)} %bitcast.5), custom_call_target="tpu_custom_call" | custom-call | tf_op jit(solution)/shard_map/geometry/pallas_call | solution.py:357
  2.5 0.0 copy-start
  2.5 9.4 %all-to-all-start = ((f32[8,8,128]{2,1,0:T(8,128)}), f32[8,8,128]{2,1,0:T(8,128)S(1)}, u32[]{:S(2)}, u32[]{:S(2)}) async-start(f32[8,8,128]{2,1,0:T(8,128)} %geometry.1), calls=%async_computation | async-start | bytes 65536 | tf_op jit(solution)/shard_map/all_to_all | solution.py:373
  11.9 0.0 copy-done
  11.9 0.1 copy.10.velocity_ref
  12.0 2.5 %all-to-all-done.rows_ref = f32[8,8,128]{2,1,0:T(8,128)S(1)} async-done(((f32[8,8,128]{2,1,0:T(8,128)}), f32[8,8,128]{2,1,0:T(8,128)S(1)}, u32[]{:S(2)}, u32[]{:S(2)}) %all-to-all-start) | async-done | bytes 32800 | tf_op jit(solution)/shard_map/all_to_all | solution.py:373
  14.5 1.8 %loads.1 = (f32[1,64,128]{2,1,0:T(8,128)}, f32[1,64,128]{2,1,0:T(8,128)}) custom-call(f32[8,8,128]{2,1,0:T(8,128)S(1)} %all-to-all-done.rows_ref, f32[64,3]{1,0:T(8,128)S(1)} %copy.10.velocity_ref), custom_call_target="tpu_custom_call" | custom-call | tf_op jit(solution)/shard_map/loads/pallas_call | solution.py:378
Async XLA Ops:
  2.5 9.4 %copy-start = (f32[64,3]{0,1:T(4,128)S(1)}, f32[64,3]{0,1:T(4,128)}, u32[]{:S(2)}) copy-start(f32[64,3]{0,1:T(4,128)} %param.15) | copy-start | bytes 2308
  2.5 12.0 %all-to-all-start = ((f32[8,8,128]{2,1,0:T(8,128)}), f32[8,8,128]{2,1,0:T(8,128)S(1)}, u32[]{:S(2)}, u32[]{:S(2)}) async-start(f32[8,8,128]{2,1,0:T(8,128)} %geometry.1), calls=%async_computation | async-start | bytes 65536 | tf_op jit(solution)/shard_map/all_to_all | solution.py:373

commit v3 on v1

--- a/solution.py
+++ b/solution.py
@@ -196,6 +196,73 @@
 
 def geometry_kernel(
     vert_dev,
+    phases,
+    order_hbm,
+    base_hbm,
+    control_hbm,
+    weights_hbm,
+    corner_hbm,
+    flags_hbm,
+    owner_hbm,
+    out_hbm,
+    order_ref,
+    base_ref,
+    control_ref,
+    weights_ref,
+    corner_ref,
+    flags_ref,
+    owner_ref,
+    out_ref,
+    arrived,
+):
+    @pl.when(lax.axis_index("phase") == 0)
+    def _():
+        sources = (
+            base_hbm,
+            control_hbm,
+            weights_hbm,
+            order_hbm,
+            corner_hbm,
+            flags_hbm,
+            owner_hbm,
+        )
+        places = (
+            base_ref,
+            control_ref,
+            weights_ref,
+            order_ref,
+            corner_ref,
+            flags_ref,
+            owner_ref,
+        )
+        copies = [
+            pltpu.make_async_copy(source, place, arrived.at[k])
+            for k, (source, place) in enumerate(zip(sources, places))
+        ]
+        for copy in copies:
+            copy.start()
+        for copy in copies:
+            copy.wait()
+        panel_rows(
+            vert_dev,
+            phases,
+            order_ref,
+            base_ref,
+            control_ref,
+            weights_ref,
+            corner_ref,
+            flags_ref,
+            owner_ref,
+            out_ref,
+        )
+        copy = pltpu.make_async_copy(out_ref, out_hbm, arrived.at[0])
+        copy.start()
+        copy.wait()
+
+
+def panel_rows(
+    vert_dev,
+    phases,
     order_ref,
     base_ref,
     control_ref,
@@ -205,7 +272,6 @@
     owner_ref,
     out_ref,
 ):
-    variant = order_ref[lax.axis_index("phase")]
     pan_dev = corner_ref.shape[1]
     diagonal = lax.broadcasted_iota(jnp.int32, (vert_dev, vert_dev), 0) == lax.broadcasted_iota(
         jnp.int32, (vert_dev, vert_dev), 1
@@ -214,7 +280,9 @@
         jnp.sum(jnp.where(diagonal, base_ref[a : a + 1, :], 0.0), axis=1, keepdims=True)
         for a in range(3)
     ]
-    totals = [jnp.zeros((vert_dev, LANES), jnp.float32) for _ in range(3)]
+    totals = [
+        [jnp.zeros((vert_dev, LANES), jnp.float32) for _ in range(3)] for _ in range(phases)
+    ]
     for start in range(0, control_ref.shape[1], LANES):
         part = pl.ds(start, LANES)
         distance = (
@@ -223,35 +291,50 @@
             + (control_ref[2:3, part] - base[2]) ** 2
         )
         basis = lax.rsqrt(1.0 + distance)
-        totals = [totals[a] + weights_ref[variant, a : a + 1, part] * basis for a in range(3)]
-    moved = [base[a] + jnp.sum(totals[a], axis=1, keepdims=True) for a in range(3)]
+        for slot in range(phases):
+            for a in range(3):
+                weights = weights_ref[a, 0:1, part]
+                for v in range(1, weights_ref.shape[1]):
+                    weights = jnp.where(
+                        order_ref[slot] == v, weights_ref[a, v : v + 1, part], weights
+                    )
+                totals[slot][a] = totals[slot][a] + weights * basis
     vertex = lax.broadcasted_iota(jnp.int32, (vert_dev, pan_dev), 0)
-    corners = []
-    for k in range(3):
-        chosen = vertex == lax.rem(corner_ref[k : k + 1, :], vert_dev)
-        corners.append(
-            [jnp.sum(jnp.where(chosen, moved[a], 0.0), axis=0, keepdims=True) for a in range(3)]
-        )
-    first, second, third = corners
-    centroid = [(first[a] + second[a] + third[a]) * (1.0 / 3.0) for a in range(3)]
-    one = [second[a] - first[a] for a in range(3)]
-    two = [third[a] - first[a] for a in range(3)]
-    area = [
-        0.5 * (one[1] * two[2] - one[2] * two[1]),
-        0.5 * (one[2] * two[0] - one[0] * two[2]),
-        0.5 * (one[0] * two[1] - one[1] * two[0]),
-    ]
+    chosen = [vertex == lax.rem(corner_ref[k : k + 1, :], vert_dev) for k in range(3)]
     hull = (1 - flags_ref[...]).astype(jnp.float32)
     owner = owner_ref[...].astype(jnp.float32)
-    rows = jnp.concatenate(centroid + area + [hull, owner], axis=0)
-    rows = jnp.concatenate([rows] * (LANES // pan_dev), axis=1)
-    last = lax.broadcasted_iota(jnp.int32, rows.shape, 0) == rows.shape[0] - 1
-    for target in range(out_ref.shape[0]):
-        out_ref[target] = jnp.where(last, rows - float(target), rows)
-
-
-def loads_kernel(pan_dev, kernel_scale, rows_ref, velocity_ref, shear_ref, moment_ref, influence):
-    owners = rows_ref.shape[0]
+    targets = out_ref.shape[0]
+    for slot in range(phases):
+        moved = [base[a] + jnp.sum(totals[slot][a], axis=1, keepdims=True) for a in range(3)]
+        first, second, third = [
+            [
+                jnp.sum(jnp.where(chosen[k], moved[a], 0.0), axis=0, keepdims=True)
+                for a in range(3)
+            ]
+            for k in range(3)
+        ]
+        centroid = [(first[a] + second[a] + third[a]) * (1.0 / 3.0) for a in range(3)]
+        one = [second[a] - first[a] for a in range(3)]
+        two = [third[a] - first[a] for a in range(3)]
+        area = [
+            0.5 * (one[1] * two[2] - one[2] * two[1]),
+            0.5 * (one[2] * two[0] - one[0] * two[2]),
+            0.5 * (one[0] * two[1] - one[1] * two[0]),
+        ]
+        rows = jnp.concatenate(centroid + area + [hull, owner], axis=0)
+        rows = jnp.concatenate([rows] * (LANES // pan_dev), axis=1)
+        last = lax.broadcasted_iota(jnp.int32, rows.shape, 0) == rows.shape[0] - 1
+        for target in range(targets // phases):
+            out_ref[targets - 1 - target * phases - slot] = jnp.where(
+                last, rows - float(target), rows
+            )
+
+
+def loads_kernel(
+    pan_dev, phases, kernel_scale, rows_ref, velocity_ref, shear_ref, moment_ref, influence
+):
+    members = rows_ref.shape[0]
+    owners = members // phases
     shared = LANES // pan_dev
     tiles = owners // shared
     panels_total = owners * pan_dev
@@ -259,9 +342,9 @@
     lane = lax.broadcasted_iota(jnp.int32, (8, LANES), 1)
     panels, columns = [], []
     for q in range(tiles):
-        tile = rows_ref[q * shared]
+        tile = rows_ref[members - 1 - q * shared * phases]
         for h in range(1, shared):
-            tile = jnp.where(lane >= h * pan_dev, rows_ref[q * shared + h], tile)
+            tile = jnp.where(lane >= h * pan_dev, rows_ref[members - 1 - (q * shared + h) * phases], tile)
         panels.append(tile)
         area = [tile[3 + a : 4 + a, :] for a in range(3)]
         weight = jnp.sqrt(area[0] * area[0] + area[1] * area[1] + area[2] * area[2] + SKIN_SQUARE)
@@ -349,27 +432,46 @@
     pan_dev = connectivity.shape[1]
     load_count = load_velocity.shape[0]
     panels_total = pan_dev * owners
+    phases = lax.axis_size("phase")
+    members = owners * phases
+    variants = morph_weights.shape[0]
+    control = control_points.shape[1]
     vmem = pl.BlockSpec(memory_space=pltpu.VMEM)
+    anywhere = pl.BlockSpec(memory_space=pl.ANY)
     rows = pl.pallas_call(
-        functools.partial(geometry_kernel, vert_dev),
-        out_shape=jax.ShapeDtypeStruct((owners, 8, LANES), jnp.float32),
-        in_specs=[pl.BlockSpec(memory_space=pltpu.SMEM)] + [vmem] * 6,
-        out_specs=vmem,
+        functools.partial(geometry_kernel, vert_dev, phases),
+        out_shape=jax.ShapeDtypeStruct((members, 8, LANES), jnp.float32),
+        in_specs=[anywhere] * 7,
+        out_specs=anywhere,
+        scratch_shapes=[
+            pltpu.SMEM((variants,), jnp.int32),
+            pltpu.VMEM((3, vert_dev), jnp.float32),
+            pltpu.VMEM((3, control), jnp.float32),
+            pltpu.VMEM((3, variants, control), jnp.float32),
+            pltpu.VMEM((3, pan_dev), jnp.int32),
+            pltpu.VMEM((1, pan_dev), jnp.int32),
+            pltpu.VMEM((1, pan_dev), jnp.int32),
+            pltpu.VMEM((members, 8, LANES), jnp.float32),
+            pltpu.SemaphoreType.DMA((7,)),
+        ],
         name="geometry",
     )(
         variant_order,
         base_points,
         control_points,
-        morph_weights,
+        morph_weights.transpose(1, 0, 2),
         connectivity,
         free_flags.reshape(1, pan_dev),
         station_owner.reshape(1, pan_dev),
     )
-    rows = lax.all_to_all(rows, ("panels", "cols"), split_axis=0, concat_axis=0)
+    order = list(range(members))[::-1]
+    rows = lax.all_to_all(
+        rows, ("panels", "cols", "phase"), split_axis=0, concat_axis=0, axis_index_groups=[order]
+    )
     kernel_scale = 1.0 / (4.0 * math.pi * math.sqrt(panels_total))
     out = jax.ShapeDtypeStruct((1, load_count, STATIONS), jnp.float32)
     return pl.pallas_call(
-        functools.partial(loads_kernel, pan_dev, kernel_scale),
+        functools.partial(loads_kernel, pan_dev, phases, kernel_scale),
         out_shape=(out, out),
         in_specs=[vmem] * 2,
         out_specs=(vmem, vmem),

time: 20.2 us -> 16 us (0.79)
  waiting for transfers between devices: 6.58 us -> 3.61 us
  local copies, waits for them, and re-layouts: 1.55 us -> 0.1 us
    all_to_all x1, waiting for transfers between devices: 6.58 us -> 3.61 us  [shards_whole(): lax.all_to_all(rows, ('panels', 'cols', 'phase'), split_axis=0, concat_ax...]
    unnamed x4 -> x3, local copies, waits for them, and re-layouts: 1.55 us -> 0.1 us
  transfers between devices with their start and end apart: 1 -> 1, of which waited for: 1 -> 1; matrix products, arithmetic and copies ran while one was open for 0% -> 1% of each run, Pallas kernels for 0% -> 0%
where the time goes in v3:
time: 16 us; the launch traced here: 15.7 us
  starting transfers between devices  7.57 us (47%)
  Pallas kernels  3.8 us (24%)
  waiting for transfers between devices  3.61 us (23%)
  between operations  0.65 us (4%)
    all_to_all x1, starting transfers between devices, shards_whole(): lax.all_to_all(rows, ('panels', 'cols', 'phase'), split_axis=0, concat_ax...  7.57 us
    all_to_all x1, waiting for transfers between devices, shards_whole(): lax.all_to_all(rows, ('panels', 'cols', 'phase'), split_axis=0, concat_ax...  3.61 us
    pallas_call x1, Pallas kernels, shards_whole(): pl.pallas_call(functools.partial(geometry_kernel, vert_dev, phases), out_...  1.99 us
    pallas_call x1, Pallas kernels, shards_whole(): pl.pallas_call(functools.partial(loads_kernel, pan_dev, phases, kernel_sc...  1.8 us
  transfers between devices with their start and end apart: 1, of which 1 were waited for; matrix products, arithmetic and copies ran while one was open for 1% of the time, Pallas kernels for 0%

profile of v3, /device:TPU:0, one launch (start us, length us, event | category | flops | bytes accessed | tf_op | source)
XLA Modules:
  0.0 15.7 jit_solution(16898568201211100380)
XLA Ops:
  0.6 2.0 %geometry.1 = f32[16,8,128]{2,1,0:T(8,128)} custom-call(s32[2]{0:T(128)} %order_hbm.1, f32[3,32]{1,0:T(4,128)} %base_hbm.1, f32[3,2048]{1,0:T(4,128)} %control_hbm.1, f32[3,2,2048]{2,1,0:T(2,128)} %bitcast.3, s32[3,64]{1,0:T(4,128)} %corner_hbm.1, s32[1,64]{1,0:T(1,128)} %bitcast.4, s32[1,64]{1,0:T(1,128)} %bitcast.5), custom_call_target="tpu_custom_call" | custom-call | tf_op jit(solution)/shard_map/geometry/pallas_call | solution.py:441
  2.6 0.0 copy-start
  2.6 7.6 %all-to-all-start = ((f32[16,8,128]{2,1,0:T(8,128)}), f32[16,8,128]{2,1,0:T(8,128)S(1)}, u32[]{:S(2)}, u32[]{:S(2)}) async-start(f32[16,8,128]{2,1,0:T(8,128)} %geometry.1), calls=%async_computation | async-start | bytes 131072 | tf_op jit(solution)/shard_map/all_to_all | solution.py:468
  10.2 0.0 copy-done
  10.2 0.1 copy.10.velocity_ref
  10.3 3.6 %all-to-all-done.rows_ref = f32[16,8,128]{2,1,0:T(8,128)S(1)} async-done(((f32[16,8,128]{2,1,0:T(8,128)}), f32[16,8,128]{2,1,0:T(8,128)S(1)}, u32[]{:S(2)}, u32[]{:S(2)}) %all-to-all-start) | async-done | bytes 65568 | tf_op jit(solution)/shard_map/all_to_all | solution.py:468
  13.9 1.8 %loads.1 = (f32[1,64,128]{2,1,0:T(8,128)}, f32[1,64,128]{2,1,0:T(8,128)}) custom-call(f32[16,8,128]{2,1,0:T(8,128)S(1)} %all-to-all-done.rows_ref, f32[64,3]{1,0:T(8,128)S(1)} %copy.10.velocity_ref), custom_call_target="tpu_custom_call" | custom-call | tf_op jit(solution)/shard_map/loads/pallas_call | solution.py:473
Async XLA Ops:
  2.6 7.6 %copy-start = (f32[64,3]{0,1:T(4,128)S(1)}, f32[64,3]{0,1:T(4,128)}, u32[]{:S(2)}) copy-start(f32[64,3]{0,1:T(4,128)} %param.15) | copy-start | bytes 2308
  2.6 11.3 %all-to-all-start = ((f32[16,8,128]{2,1,0:T(8,128)}), f32[16,8,128]{2,1,0:T(8,128)S(1)}, u32[]{:S(2)}, u32[]{:S(2)}) async-start(f32[16,8,128]{2,1,0:T(8,128)} %geometry.1), calls=%async_computation | async-start | bytes 131072 | tf_op jit(solution)/shard_map/all_to_all | solution.py:468

commit v4 on v3

--- a/solution.py
+++ b/solution.py
@@ -215,7 +215,7 @@
     out_ref,
     arrived,
 ):
-    @pl.when(lax.axis_index("phase") == 0)
+    @pl.when(lax.axis_index("phase") == phases - 1)
     def _():
         sources = (
             base_hbm,
@@ -321,11 +321,17 @@
             0.5 * (one[2] * two[0] - one[0] * two[2]),
             0.5 * (one[0] * two[1] - one[1] * two[0]),
         ]
-        rows = jnp.concatenate(centroid + area + [hull, owner], axis=0)
-        rows = jnp.concatenate([rows] * (LANES // pan_dev), axis=1)
-        last = lax.broadcasted_iota(jnp.int32, rows.shape, 0) == rows.shape[0] - 1
+        rows = centroid + area + [hull, owner]
+        height = out_ref.shape[1]
+        rows = jnp.concatenate(
+            [jnp.concatenate(rows[k : k + height], axis=0) for k in range(0, len(rows), height)],
+            axis=1,
+        )
+        last = (lax.broadcasted_iota(jnp.int32, rows.shape, 0) == height - 1) & (
+            lax.broadcasted_iota(jnp.int32, rows.shape, 1) >= LANES - pan_dev
+        )
         for target in range(targets // phases):
-            out_ref[targets - 1 - target * phases - slot] = jnp.where(
+            out_ref[targets - (target + 1) * phases + slot] = jnp.where(
                 last, rows - float(target), rows
             )
 
@@ -339,12 +345,19 @@
     tiles = owners // shared
     panels_total = owners * pan_dev
     load_count = velocity_ref.shape[0]
-    lane = lax.broadcasted_iota(jnp.int32, (8, LANES), 1)
+    height = rows_ref.shape[1]
+    lane = lax.broadcasted_iota(jnp.int32, (height, LANES), 1)
     panels, columns = [], []
     for q in range(tiles):
-        tile = rows_ref[members - 1 - q * shared * phases]
-        for h in range(1, shared):
-            tile = jnp.where(lane >= h * pan_dev, rows_ref[members - 1 - (q * shared + h) * phases], tile)
+        blocks = [rows_ref[members - 1 - (q * shared + h) * phases] for h in range(shared)]
+        pieces = []
+        for k in range(shared):
+            piece = None
+            for h, block in enumerate(blocks):
+                moved = block if h == k else pltpu.roll(block, (h - k) % shared * pan_dev, 1)
+                piece = moved if h == 0 else jnp.where(lane >= h * pan_dev, moved, piece)
+            pieces.append(piece)
+        tile = jnp.concatenate(pieces, axis=0)
         panels.append(tile)
         area = [tile[3 + a : 4 + a, :] for a in range(3)]
         weight = jnp.sqrt(area[0] * area[0] + area[1] * area[1] + area[2] * area[2] + SKIN_SQUARE)
@@ -436,11 +449,12 @@
     members = owners * phases
     variants = morph_weights.shape[0]
     control = control_points.shape[1]
+    height = 8 * pan_dev // LANES
     vmem = pl.BlockSpec(memory_space=pltpu.VMEM)
     anywhere = pl.BlockSpec(memory_space=pl.ANY)
     rows = pl.pallas_call(
         functools.partial(geometry_kernel, vert_dev, phases),
-        out_shape=jax.ShapeDtypeStruct((members, 8, LANES), jnp.float32),
+        out_shape=jax.ShapeDtypeStruct((members, height, LANES), jnp.float32),
         in_specs=[anywhere] * 7,
         out_specs=anywhere,
         scratch_shapes=[
@@ -451,7 +465,7 @@
             pltpu.VMEM((3, pan_dev), jnp.int32),
             pltpu.VMEM((1, pan_dev), jnp.int32),
             pltpu.VMEM((1, pan_dev), jnp.int32),
-            pltpu.VMEM((members, 8, LANES), jnp.float32),
+            pltpu.VMEM((members, height, LANES), jnp.float32),
             pltpu.SemaphoreType.DMA((7,)),
         ],
         name="geometry",
@@ -464,7 +478,7 @@
         free_flags.reshape(1, pan_dev),
         station_owner.reshape(1, pan_dev),
     )
-    order = list(range(members))[::-1]
+    order = [owner * phases + k for owner in range(owners)[::-1] for k in range(phases)]
     rows = lax.all_to_all(
         rows, ("panels", "cols", "phase"), split_axis=0, concat_axis=0, axis_index_groups=[order]
     )
@@ -498,6 +512,7 @@
         panels_total <= PANELS_ON_ONE
         and panels_total % LANES == 0
         and LANES % pan_dev == 0
+        and 8 * pan_dev % LANES == 0
         and STATIONS == LANES
         and variant_order.shape[0] == lax.axis_size("phase")
         and control_points.shape[1] % LANES == 0

time: 16 us -> 15.2 us (0.950)
  Pallas kernels: 3.8 us -> 2 us
  starting transfers between devices: 7.57 us -> 9.36 us
  waiting for transfers between devices: 3.61 us -> 2.88 us
    pallas_call x1, Pallas kernels: 1.99 us -> 0.07 us  [shards_whole(): pl.pallas_call(functools.partial(geometry_kernel, vert_dev, phases), out_...]
    all_to_all x1, starting transfers between devices: 7.57 us -> 9.36 us  [shards_whole(): lax.all_to_all(rows, ('panels', 'cols', 'phase'), split_axis=0, concat_ax...]
    all_to_all x1, waiting for transfers between devices: 3.61 us -> 2.88 us  [shards_whole(): lax.all_to_all(rows, ('panels', 'cols', 'phase'), split_axis=0, concat_ax...]
where the time goes in v4:
time: 15.2 us; the launch traced here: 15 us
  starting transfers between devices  9.36 us (62%)
  waiting for transfers between devices  2.88 us (19%)
  Pallas kernels  2 us (13%)
  between operations  0.65 us (4%)
    all_to_all x1, starting transfers between devices, shards_whole(): lax.all_to_all(rows, ('panels', 'cols', 'phase'), split_axis=0, concat_ax...  9.36 us
    all_to_all x1, waiting for transfers between devices, shards_whole(): lax.all_to_all(rows, ('panels', 'cols', 'phase'), split_axis=0, concat_ax...  2.88 us
    pallas_call x1, Pallas kernels, shards_whole(): pl.pallas_call(functools.partial(loads_kernel, pan_dev, phases, kernel_sc...  1.92 us
  transfers between devices with their start and end apart: 1, of which 1 were waited for; matrix products, arithmetic and copies ran while one was open for 1% of the time, Pallas kernels for 0%

profile of v4, /device:TPU:0, one launch (start us, length us, event | category | flops | bytes accessed | tf_op | source)
XLA Modules:
  0.0 15.0 jit_solution(9499011112754472729)
XLA Ops:
  0.6 0.1 geometry.1
  0.7 0.0 copy-start
  0.7 9.4 %all-to-all-start = ((f32[16,4,128]{2,1,0:T(4,128)}), f32[16,4,128]{2,1,0:T(4,128)S(1)}, u32[]{:S(2)}, u32[]{:S(2)}) async-start(f32[16,4,128]{2,1,0:T(4,128)} %geometry.1), calls=%async_computation | async-start | bytes 65536 | tf_op jit(solution)/shard_map/all_to_all | solution.py:482
  10.1 0.0 copy-done
  10.1 0.1 copy.10.velocity_ref
  10.2 2.9 %all-to-all-done.rows_ref = f32[16,4,128]{2,1,0:T(4,128)S(1)} async-done(((f32[16,4,128]{2,1,0:T(4,128)}), f32[16,4,128]{2,1,0:T(4,128)S(1)}, u32[]{:S(2)}, u32[]{:S(2)}) %all-to-all-start) | async-done | bytes 32800 | tf_op jit(solution)/shard_map/all_to_all | solution.py:482
  13.1 1.9 %loads.1 = (f32[1,64,128]{2,1,0:T(8,128)}, f32[1,64,128]{2,1,0:T(8,128)}) custom-call(f32[16,4,128]{2,1,0:T(4,128)S(1)} %all-to-all-done.rows_ref, f32[64,3]{1,0:T(8,128)S(1)} %copy.10.velocity_ref), custom_call_target="tpu_custom_call" | custom-call | tf_op jit(solution)/shard_map/loads/pallas_call | solution.py:487
Async XLA Ops:
  0.7 9.4 %copy-start = (f32[64,3]{0,1:T(4,128)S(1)}, f32[64,3]{0,1:T(4,128)}, u32[]{:S(2)}) copy-start(f32[64,3]{0,1:T(4,128)} %param.15) | copy-start | bytes 2308
  0.7 12.3 %all-to-all-start = ((f32[16,4,128]{2,1,0:T(4,128)}), f32[16,4,128]{2,1,0:T(4,128)S(1)}, u32[]{:S(2)}, u32[]{:S(2)}) async-start(f32[16,4,128]{2,1,0:T(4,128)} %geometry.1), calls=%async_computation | async-start | bytes 65536 | tf_op jit(solution)/shard_map/all_to_all | solution.py:482

commit v5 on v4

--- a/solution.py
+++ b/solution.py
@@ -204,7 +204,7 @@
     corner_hbm,
     flags_hbm,
     owner_hbm,
-    out_hbm,
+    out_ref,
     order_ref,
     base_ref,
     control_ref,
@@ -212,7 +212,6 @@
     corner_ref,
     flags_ref,
     owner_ref,
-    out_ref,
     arrived,
 ):
     @pl.when(lax.axis_index("phase") == phases - 1)
@@ -255,9 +254,6 @@
             owner_ref,
             out_ref,
         )
-        copy = pltpu.make_async_copy(out_ref, out_hbm, arrived.at[0])
-        copy.start()
-        copy.wait()
 
 
 def panel_rows(
@@ -344,7 +340,7 @@
     shared = LANES // pan_dev
     tiles = owners // shared
     panels_total = owners * pan_dev
-    load_count = velocity_ref.shape[0]
+    load_count = velocity_ref.shape[1]
     height = rows_ref.shape[1]
     lane = lax.broadcasted_iota(jnp.int32, (height, LANES), 1)
     panels, columns = [], []
@@ -378,7 +374,10 @@
             influence[pl.ds(source * LANES, LANES), pl.ds(target * LANES, LANES)] = (
                 weight * lax.rsqrt(distance + CORE_SQUARE)
             ).astype(jnp.bfloat16)
-    velocity = [velocity_ref[:, a : a + 1] for a in range(3)]
+    velocity = jnp.concatenate(
+        [velocity_ref[...], jnp.zeros((8 - velocity_ref.shape[0], load_count), jnp.float32)], axis=0
+    ).T
+    velocity = [velocity[:, a : a + 1] for a in range(3)]
     boundary = jnp.concatenate(
         [
             (velocity[0] * tile[3:4, :] + velocity[1] * tile[4:5, :] + velocity[2] * tile[5:6, :])
@@ -454,9 +453,9 @@
     anywhere = pl.BlockSpec(memory_space=pl.ANY)
     rows = pl.pallas_call(
         functools.partial(geometry_kernel, vert_dev, phases),
-        out_shape=jax.ShapeDtypeStruct((members, height, LANES), jnp.float32),
+        out_shape=pltpu.VMEM((members, height, LANES), jnp.float32),
         in_specs=[anywhere] * 7,
-        out_specs=anywhere,
+        out_specs=vmem,
         scratch_shapes=[
             pltpu.SMEM((variants,), jnp.int32),
             pltpu.VMEM((3, vert_dev), jnp.float32),
@@ -465,7 +464,6 @@
             pltpu.VMEM((3, pan_dev), jnp.int32),
             pltpu.VMEM((1, pan_dev), jnp.int32),
             pltpu.VMEM((1, pan_dev), jnp.int32),
-            pltpu.VMEM((members, height, LANES), jnp.float32),
             pltpu.SemaphoreType.DMA((7,)),
         ],
         name="geometry",
@@ -492,7 +490,7 @@
         scratch_shapes=[pltpu.VMEM((panels_total, panels_total), jnp.bfloat16)],
         compiler_params=pltpu.CompilerParams(vmem_limit_bytes=32 * 1024 * 1024),
         name="loads",
-    )(rows, load_velocity)
+    )(rows, load_velocity.T)
 
 
 def shards(

time: 15.2 us -> 13.7 us (0.901)
  blocking collectives: 0 us -> 10.9 us
  starting transfers between devices: 9.36 us -> 0 us
  waiting for transfers between devices: 2.88 us -> 0 us
    all_to_all x0 -> x1, blocking collectives: none -> 10.9 us  [shards_whole(): lax.all_to_all(rows, ('panels', 'cols', 'phase'), split_axis=0, concat_ax...]
    all_to_all x1 -> x0, starting transfers between devices: 9.36 us -> none  [shards_whole(): lax.all_to_all(rows, ('panels', 'cols', 'phase'), split_axis=0, concat_ax...]
    all_to_all x1 -> x0, waiting for transfers between devices: 2.88 us -> none  [shards_whole(): lax.all_to_all(rows, ('panels', 'cols', 'phase'), split_axis=0, concat_ax...]
  transfers between devices with their start and end apart: 1 -> 0, of which waited for: 1 -> 0; matrix products, arithmetic and copies ran while one was open for 1% -> 0% of each run, Pallas kernels for 0% -> 0%
where the time goes in v5:
time: 13.7 us; the launch traced here: 13.6 us
  blocking collectives  10.9 us (80%)
  Pallas kernels  1.97 us (14%)
  between operations  0.65 us (5%)
    all_to_all x1, blocking collectives, shards_whole(): lax.all_to_all(rows, ('panels', 'cols', 'phase'), split_axis=0, concat_ax...  10.9 us
    pallas_call x1, Pallas kernels, shards_whole(): pl.pallas_call(functools.partial(loads_kernel, pan_dev, phases, kernel_sc...  1.89 us

profile of v5, /device:TPU:0, one launch (start us, length us, event | category | flops | bytes accessed | tf_op | source)
XLA Modules:
  0.0 13.6 jit_solution(3372516915652778980)
XLA Ops:
  0.6 0.1 geometry.1
  0.7 0.0 copy-start
  0.7 10.9 %all_to_all.5.rows_ref = f32[16,4,128]{2,1,0:T(4,128)S(1)} all-to-all(f32[16,4,128]{2,1,0:T(4,128)S(1)} %geometry.1), channel_id=1, replica_groups={{14,15,12,13,10,11,8,9,6,7,4,5,2,3,0,1},{30,31,28,29,26,27,24,25,22,23,..., dimensions={0} | all-to-all | bytes 65536 | tf_op jit(solution)/shard_map/all_to_all | solution.py:480
  11.7 0.0 copy-done
  11.7 1.9 %loads.1 = (f32[1,64,128]{2,1,0:T(8,128)}, f32[1,64,128]{2,1,0:T(8,128)}) custom-call(f32[16,4,128]{2,1,0:T(4,128)S(1)} %all_to_all.5.rows_ref, f32[3,64]{1,0:T(4,128)S(1)} %bitcast.4), custom_call_target="tpu_custom_call" | custom-call | tf_op jit(solution)/shard_map/loads/pallas_call | solution.py:485
Async XLA Ops:
  0.7 11.0 %copy-start = (f32[64,3]{0,1:T(4,128)S(1)}, f32[64,3]{0,1:T(4,128)}, u32[]{:S(2)}) copy-start(f32[64,3]{0,1:T(4,128)} %param.15) | copy-start | bytes 2308

commit v6 on v5

--- a/solution.py
+++ b/solution.py
@@ -3,6 +3,7 @@
 
 import jax
 import jax.numpy as jnp
+import numpy as np
 from jax import lax
 from jax.experimental import pallas as pl
 from jax.experimental.pallas import tpu as pltpu
@@ -197,6 +198,7 @@
 def geometry_kernel(
     vert_dev,
     phases,
+    order,
     order_hbm,
     base_hbm,
     control_hbm,
@@ -217,22 +219,22 @@
     @pl.when(lax.axis_index("phase") == phases - 1)
     def _():
         sources = (
+            weights_hbm,
+            control_hbm,
             base_hbm,
-            control_hbm,
-            weights_hbm,
-            order_hbm,
             corner_hbm,
             flags_hbm,
             owner_hbm,
+            order_hbm,
         )
         places = (
+            weights_ref,
+            control_ref,
             base_ref,
-            control_ref,
-            weights_ref,
-            order_ref,
             corner_ref,
             flags_ref,
             owner_ref,
+            order_ref,
         )
         copies = [
             pltpu.make_async_copy(source, place, arrived.at[k])
@@ -245,6 +247,7 @@
         panel_rows(
             vert_dev,
             phases,
+            order,
             order_ref,
             base_ref,
             control_ref,
@@ -259,6 +262,7 @@
 def panel_rows(
     vert_dev,
     phases,
+    order,
     order_ref,
     base_ref,
     control_ref,
@@ -269,6 +273,7 @@
     out_ref,
 ):
     pan_dev = corner_ref.shape[1]
+    variants = weights_ref.shape[1]
     diagonal = lax.broadcasted_iota(jnp.int32, (vert_dev, vert_dev), 0) == lax.broadcasted_iota(
         jnp.int32, (vert_dev, vert_dev), 1
     )
@@ -276,9 +281,7 @@
         jnp.sum(jnp.where(diagonal, base_ref[a : a + 1, :], 0.0), axis=1, keepdims=True)
         for a in range(3)
     ]
-    totals = [
-        [jnp.zeros((vert_dev, LANES), jnp.float32) for _ in range(3)] for _ in range(phases)
-    ]
+    totals = [[None] * 3 for _ in range(variants)]
     for start in range(0, control_ref.shape[1], LANES):
         part = pl.ds(start, LANES)
         distance = (
@@ -287,65 +290,108 @@
             + (control_ref[2:3, part] - base[2]) ** 2
         )
         basis = lax.rsqrt(1.0 + distance)
-        for slot in range(phases):
+        for v in range(variants):
             for a in range(3):
-                weights = weights_ref[a, 0:1, part]
-                for v in range(1, weights_ref.shape[1]):
-                    weights = jnp.where(
-                        order_ref[slot] == v, weights_ref[a, v : v + 1, part], weights
-                    )
-                totals[slot][a] = totals[slot][a] + weights * basis
-    vertex = lax.broadcasted_iota(jnp.int32, (vert_dev, pan_dev), 0)
-    chosen = [vertex == lax.rem(corner_ref[k : k + 1, :], vert_dev) for k in range(3)]
-    hull = (1 - flags_ref[...]).astype(jnp.float32)
-    owner = owner_ref[...].astype(jnp.float32)
-    targets = out_ref.shape[0]
+                term = weights_ref[a, v : v + 1, part] * basis
+                totals[v][a] = term if start == 0 else totals[v][a] + term
+    lane = lax.broadcasted_iota(jnp.int32, (vert_dev, LANES), 1)
+    moved = []
+    for a in range(3):
+        shift = jnp.sum(totals[0][a], axis=1, keepdims=True)
+        for v in range(1, variants):
+            own = jnp.sum(totals[v][a], axis=1, keepdims=True)
+            shift = jnp.where(lane >= v * pan_dev, own, shift)
+        moved.append(base[a] + shift)
+
+    def repeated(row):
+        return jnp.concatenate([row] * variants, axis=1)
+
+    vertex = lax.broadcasted_iota(jnp.int32, (vert_dev, LANES), 0)
+    corners = []
+    for k in range(3):
+        chosen = vertex == lax.rem(repeated(corner_ref[k : k + 1, :]), vert_dev)
+        corners.append(
+            [jnp.sum(jnp.where(chosen, moved[a], 0.0), axis=0, keepdims=True) for a in range(3)]
+        )
+    first, second, third = corners
+    centroid = [(first[a] + second[a] + third[a]) * (1.0 / 3.0) for a in range(3)]
+    one = [second[a] - first[a] for a in range(3)]
+    two = [third[a] - first[a] for a in range(3)]
+    area = [
+        0.5 * (one[1] * two[2] - one[2] * two[1]),
+        0.5 * (one[2] * two[0] - one[0] * two[2]),
+        0.5 * (one[0] * two[1] - one[1] * two[0]),
+    ]
+    hull = (1 - repeated(flags_ref[...])).astype(jnp.float32)
+    owner = repeated(owner_ref[...]).astype(jnp.float32)
+    rows = centroid + area + [hull, owner]
+    height = out_ref.shape[1]
+    shared = LANES // pan_dev
+    pieces = [jnp.concatenate(rows[k : k + height], axis=0) for k in range(0, len(rows), height)]
+    lane = lax.broadcasted_iota(jnp.int32, (height, LANES), 1)
+    last = (lax.broadcasted_iota(jnp.int32, (height, LANES), 0) == height - 1) & (
+        lane >= LANES - pan_dev
+    )
+    blocks = []
+    for v in range(variants):
+        block = None
+        for k, piece in enumerate(pieces):
+            piece = piece if k == v else pltpu.roll(piece, (k - v) % shared * pan_dev, 1)
+            block = piece if k == 0 else jnp.where(lane >= k * pan_dev, piece, block)
+        blocks.append(block)
     for slot in range(phases):
-        moved = [base[a] + jnp.sum(totals[slot][a], axis=1, keepdims=True) for a in range(3)]
-        first, second, third = [
-            [
-                jnp.sum(jnp.where(chosen[k], moved[a], 0.0), axis=0, keepdims=True)
-                for a in range(3)
-            ]
-            for k in range(3)
-        ]
-        centroid = [(first[a] + second[a] + third[a]) * (1.0 / 3.0) for a in range(3)]
-        one = [second[a] - first[a] for a in range(3)]
-        two = [third[a] - first[a] for a in range(3)]
-        area = [
-            0.5 * (one[1] * two[2] - one[2] * two[1]),
-            0.5 * (one[2] * two[0] - one[0] * two[2]),
-            0.5 * (one[0] * two[1] - one[1] * two[0]),
-        ]
-        rows = centroid + area + [hull, owner]
-        height = out_ref.shape[1]
-        rows = jnp.concatenate(
-            [jnp.concatenate(rows[k : k + height], axis=0) for k in range(0, len(rows), height)],
-            axis=1,
-        )
-        last = (lax.broadcasted_iota(jnp.int32, rows.shape, 0) == height - 1) & (
-            lax.broadcasted_iota(jnp.int32, rows.shape, 1) >= LANES - pan_dev
-        )
-        for target in range(targets // phases):
-            out_ref[targets - (target + 1) * phases + slot] = jnp.where(
-                last, rows - float(target), rows
-            )
+        block = blocks[0]
+        for v in range(1, variants):
+            block = jnp.where(order_ref[slot] == v, blocks[v], block)
+        for place, member in enumerate(order):
+            if member % phases == slot:
+                out_ref[place] = jnp.where(last, block - float(member // phases), block)
+
+
+def in_parts(values):
+    high = values.astype(jnp.bfloat16).astype(jnp.float32)
+    rest = values - high
+    middle = rest.astype(jnp.bfloat16).astype(jnp.float32)
+    return high, middle, rest - middle
+
+
+def dot_rows(left, right):
+    return lax.dot_general(
+        left.astype(jnp.bfloat16),
+        right.astype(jnp.bfloat16),
+        (((0,), (0,)), ((), ())),
+        preferred_element_type=jnp.float32,
+    )
+
+
+def spread_matrix():
+    spread = np.zeros((16, 4 * LANES), np.float32)
+    for row in range(12):
+        spread[row, row % 4 * LANES : (row % 4 + 1) * LANES] = 1.0
+    return spread
 
 
 def loads_kernel(
-    pan_dev, phases, kernel_scale, rows_ref, velocity_ref, shear_ref, moment_ref, influence
+    pan_dev,
+    places,
+    kernel_scale,
+    rows_ref,
+    velocity_ref,
+    spread_ref,
+    shear_ref,
+    moment_ref,
+    influence,
 ):
-    members = rows_ref.shape[0]
-    owners = members // phases
+    owners = len(places)
     shared = LANES // pan_dev
     tiles = owners // shared
     panels_total = owners * pan_dev
     load_count = velocity_ref.shape[1]
     height = rows_ref.shape[1]
     lane = lax.broadcasted_iota(jnp.int32, (height, LANES), 1)
-    panels, columns = [], []
+    panels = []
     for q in range(tiles):
-        blocks = [rows_ref[members - 1 - (q * shared + h) * phases] for h in range(shared)]
+        blocks = [rows_ref[places[q * shared + h]] for h in range(shared)]
         pieces = []
         for k in range(shared):
             piece = None
@@ -353,44 +399,58 @@
                 moved = block if h == k else pltpu.roll(block, (h - k) % shared * pan_dev, 1)
                 piece = moved if h == 0 else jnp.where(lane >= h * pan_dev, moved, piece)
             pieces.append(piece)
-        tile = jnp.concatenate(pieces, axis=0)
-        panels.append(tile)
-        area = [tile[3 + a : 4 + a, :] for a in range(3)]
-        weight = jnp.sqrt(area[0] * area[0] + area[1] * area[1] + area[2] * area[2] + SKIN_SQUARE)
-        columns.append(
-            jnp.concatenate([tile[0:3, :], weight * kernel_scale, tile[4:8, :]], axis=0).T
-        )
+        panels.append(jnp.concatenate(pieces, axis=0))
+    rows = jnp.concatenate(panels, axis=1)
+    centre = rows[0:3, :]
+    area = rows[3:6, :]
+    hull = rows[6:7, :]
+    owner = rows[7:8, :]
+    weight = (
+        jnp.sqrt(
+            area[0:1, :] * area[0:1, :]
+            + area[1:2, :] * area[1:2, :]
+            + area[2:3, :] * area[2:3, :]
+            + SKIN_SQUARE
+        )
+        * kernel_scale
+    )
+    high, middle, low = in_parts(jnp.concatenate([centre, weight], axis=0))
+    columns = dot_rows(
+        jnp.concatenate([high, middle, low, jnp.zeros_like(low)], axis=0), spread_ref[...]
+    )
+    blank = jnp.zeros((1, panels_total), jnp.float32)
+    area_parts = in_parts(jnp.concatenate([area, blank], axis=0))
+    velocity_parts = in_parts(
+        jnp.concatenate([velocity_ref[...], jnp.zeros((1, load_count), jnp.float32)], axis=0)
+    )
+    pairs = ((0, 0), (0, 1), (1, 0), (1, 1), (0, 2), (2, 0), (1, 2), (2, 1))
+    boundary = (
+        dot_rows(
+            jnp.concatenate([velocity_parts[k] for k, _ in pairs], axis=0),
+            jnp.concatenate([area_parts[k] for _, k in pairs], axis=0),
+        )
+        * hull
+    )
+    first = boundary.astype(jnp.bfloat16)
     for source in range(tiles):
-        column = columns[source]
-        centre = [column[:, a : a + 1] for a in range(3)]
-        weight = column[:, 3:4]
-        for target in range(tiles):
+        for target in range(source, tiles):
             tile = panels[target]
-            distance = (
-                (tile[0:1, :] - centre[0]) ** 2
-                + (tile[1:2, :] - centre[1]) ** 2
-                + (tile[2:3, :] - centre[2]) ** 2
+            column = columns[source * LANES : (source + 1) * LANES, :]
+            column = [column[:, a * LANES : (a + 1) * LANES] for a in range(4)]
+            inverse = lax.rsqrt(
+                (tile[0:1, :] - column[0]) ** 2
+                + (tile[1:2, :] - column[1]) ** 2
+                + (tile[2:3, :] - column[2]) ** 2
+                + CORE_SQUARE
             )
-            influence[pl.ds(source * LANES, LANES), pl.ds(target * LANES, LANES)] = (
-                weight * lax.rsqrt(distance + CORE_SQUARE)
-            ).astype(jnp.bfloat16)
-    velocity = jnp.concatenate(
-        [velocity_ref[...], jnp.zeros((8 - velocity_ref.shape[0], load_count), jnp.float32)], axis=0
-    ).T
-    velocity = [velocity[:, a : a + 1] for a in range(3)]
-    boundary = jnp.concatenate(
-        [
-            (velocity[0] * tile[3:4, :] + velocity[1] * tile[4:5, :] + velocity[2] * tile[5:6, :])
-            * tile[6:7, :]
-            for tile in panels
-        ],
-        axis=1,
-    )
-    first = boundary.astype(jnp.bfloat16)
+            here, there = pl.ds(source * LANES, LANES), pl.ds(target * LANES, LANES)
+            influence[here, there] = (column[3] * inverse).astype(jnp.bfloat16)
+            if target != source:
+                other = columns[target * LANES : (target + 1) * LANES, 3 * LANES :]
+                influence[there, here] = (other * inverse.T).astype(jnp.bfloat16)
     induced = jnp.dot(first, influence[...], preferred_element_type=jnp.float32)
     second = (first.astype(jnp.float32) + (boundary - induced)).astype(jnp.bfloat16)
     pressure = jnp.dot(second, influence[...], preferred_element_type=jnp.float32)
-
     stations_all = STATIONS * owners
     own_loads = jnp.zeros((load_count, LANES), jnp.float32)
     prior_loads = jnp.zeros((load_count, LANES), jnp.float32)
@@ -449,10 +509,11 @@
     variants = morph_weights.shape[0]
     control = control_points.shape[1]
     height = 8 * pan_dev // LANES
+    order = [owner * phases + k for owner in range(owners)[::-1] for k in range(phases)]
     vmem = pl.BlockSpec(memory_space=pltpu.VMEM)
     anywhere = pl.BlockSpec(memory_space=pl.ANY)
     rows = pl.pallas_call(
-        functools.partial(geometry_kernel, vert_dev, phases),
+        functools.partial(geometry_kernel, vert_dev, phases, order),
         out_shape=pltpu.VMEM((members, height, LANES), jnp.float32),
         in_specs=[anywhere] * 7,
         out_specs=vmem,
@@ -476,21 +537,25 @@
         free_flags.reshape(1, pan_dev),
         station_owner.reshape(1, pan_dev),
     )
-    order = [owner * phases + k for owner in range(owners)[::-1] for k in range(phases)]
     rows = lax.all_to_all(
         rows, ("panels", "cols", "phase"), split_axis=0, concat_axis=0, axis_index_groups=[order]
     )
+    places = [order.index(owner * phases + phases - 1) for owner in range(owners)]
     kernel_scale = 1.0 / (4.0 * math.pi * math.sqrt(panels_total))
     out = jax.ShapeDtypeStruct((1, load_count, STATIONS), jnp.float32)
     return pl.pallas_call(
-        functools.partial(loads_kernel, pan_dev, phases, kernel_scale),
+        functools.partial(loads_kernel, pan_dev, places, kernel_scale),
         out_shape=(out, out),
-        in_specs=[vmem] * 2,
+        in_specs=[vmem] * 3,
         out_specs=(vmem, vmem),
         scratch_shapes=[pltpu.VMEM((panels_total, panels_total), jnp.bfloat16)],
         compiler_params=pltpu.CompilerParams(vmem_limit_bytes=32 * 1024 * 1024),
         name="loads",
-    )(rows, load_velocity.T)
+    )(
+        rows,
+        load_velocity.T,
+        jnp.asarray(spread_matrix(), jnp.bfloat16),
+    )
 
 
 def shards(
@@ -513,6 +578,7 @@
         and 8 * pan_dev % LANES == 0
         and STATIONS == LANES
         and variant_order.shape[0] == lax.axis_size("phase")
+        and morph_weights.shape[0] * pan_dev == LANES
         and control_points.shape[1] % LANES == 0
         and load_velocity.shape[0] % 16 == 0
     )

time: 13.7 us -> 13.6 us (level)
  Pallas kernels: 1.97 us -> 1.81 us
    pallas_call x2, Pallas kernels: 1.97 us -> 1.81 us  [the longest x1 1.74 us: shards_whole(): pl.pallas_call(functools.partial(loads_kernel, pan_dev, places, kernel_sc...]
where the time goes in v6:
time: 13.6 us; the launch traced here: 13.4 us
  blocking collectives  10.9 us (80%)
  Pallas kernels  1.81 us (13%)
  between operations  0.66 us (5%)
    all_to_all x1, blocking collectives, shards_whole(): lax.all_to_all(rows, ('panels', 'cols', 'phase'), split_axis=0, concat_ax...  10.9 us
    pallas_call x1, Pallas kernels, shards_whole(): pl.pallas_call(functools.partial(loads_kernel, pan_dev, places, kernel_sc...  1.74 us

profile of v6, /device:TPU:0, one launch (start us, length us, event | category | flops | bytes accessed | tf_op | source)
XLA Modules:
  0.0 13.4 jit_solution(245613588055877751)
XLA Ops:
  0.6 0.1 geometry.1
  0.7 0.0 copy-start
  0.7 0.0 copy-start.1
  0.7 10.9 %all_to_all.5.rows_ref = f32[16,4,128]{2,1,0:T(4,128)S(1)} all-to-all(f32[16,4,128]{2,1,0:T(4,128)S(1)} %geometry.1), channel_id=1, replica_groups={{14,15,12,13,10,11,8,9,6,7,4,5,2,3,0,1},{30,31,28,29,26,27,24,25,22,23,..., dimensions={0} | all-to-all | bytes 65536 | tf_op jit(solution)/shard_map/all_to_all | solution.py:540
  11.7 0.0 copy-done
  11.7 0.0 copy-done.1
  11.7 1.7 %loads.1 = (f32[1,64,128]{2,1,0:T(8,128)}, f32[1,64,128]{2,1,0:T(8,128)}) custom-call(f32[16,4,128]{2,1,0:T(4,128)S(1)} %all_to_all.5.rows_ref, f32[3,64]{1,0:T(4,128)S(1)} %bitcast.4, bf16[16,512]{1,0:T(8,128)(2,1)S(1)} %copy-done), custom_call_target="tpu_custom_call" | custom-call | tf_op jit(solution)/shard_map/loads/pallas_call | solution.py:546
Async XLA Ops:
  0.7 11.0 %copy-start = (bf16[16,512]{1,0:T(8,128)(2,1)S(1)}, bf16[16,512]{1,0:T(8,128)(2,1)}, u32[]{:S(2)}) copy-start(bf16[16,512]{1,0:T(8,128)(2,1)} %constant.2.clone.spread_ref) | copy-start | bytes 49156
  0.7 11.0 %copy-start.1 = (f32[64,3]{0,1:T(4,128)S(1)}, f32[64,3]{0,1:T(4,128)}, u32[]{:S(2)}) copy-start(f32[64,3]{0,1:T(4,128)} %param.16) | copy-start | bytes 2308

commit v7 on v6

--- a/solution.py
+++ b/solution.py
@@ -199,6 +199,7 @@
     vert_dev,
     phases,
     order,
+    kernel_scale,
     order_hbm,
     base_hbm,
     control_hbm,
@@ -248,6 +249,7 @@
             vert_dev,
             phases,
             order,
+            kernel_scale,
             order_ref,
             base_ref,
             control_ref,
@@ -263,6 +265,7 @@
     vert_dev,
     phases,
     order,
+    kernel_scale,
     order_ref,
     base_ref,
     control_ref,
@@ -322,23 +325,35 @@
         0.5 * (one[2] * two[0] - one[0] * two[2]),
         0.5 * (one[0] * two[1] - one[1] * two[0]),
     ]
+    weight = (
+        jnp.sqrt(area[0] * area[0] + area[1] * area[1] + area[2] * area[2] + SKIN_SQUARE)
+        * kernel_scale
+    )
     hull = (1 - repeated(flags_ref[...])).astype(jnp.float32)
     owner = repeated(owner_ref[...]).astype(jnp.float32)
-    rows = centroid + area + [hull, owner]
+    rows = centroid + [weight] + [hull * area[a] for a in range(3)] + [owner]
     height = out_ref.shape[1]
     shared = LANES // pan_dev
     pieces = [jnp.concatenate(rows[k : k + height], axis=0) for k in range(0, len(rows), height)]
+    turned = [
+        [pltpu.roll(piece, t * pan_dev, 1) if t else piece for t in range(shared)]
+        for piece in pieces
+    ]
     lane = lax.broadcasted_iota(jnp.int32, (height, LANES), 1)
-    last = (lax.broadcasted_iota(jnp.int32, (height, LANES), 0) == height - 1) & (
-        lane >= LANES - pan_dev
-    )
-    blocks = []
-    for v in range(variants):
-        block = None
-        for k, piece in enumerate(pieces):
-            piece = piece if k == v else pltpu.roll(piece, (k - v) % shared * pan_dev, 1)
-            block = piece if k == 0 else jnp.where(lane >= k * pan_dev, piece, block)
-        blocks.append(block)
+    row = lax.broadcasted_iota(jnp.int32, (height, LANES), 0)
+    cols = lax.axis_size("cols")
+    place_here = (lax.axis_index("panels") * cols + lax.axis_index("cols")) % shared
+    begin = (place_here + shared - 1) % shared * pan_dev
+    last = (row == height - 1) & (lane >= begin) & (lane < begin + pan_dev)
+    blocks = [None] * variants
+    for h in range(shared):
+        slots = [(k + h) % shared for k in range(shared)]
+        for v in range(variants):
+            block = turned[slots.index(0)][-v % shared]
+            for slot in range(1, shared):
+                piece = turned[slots.index(slot)][(slot - v) % shared]
+                block = jnp.where(lane >= slot * pan_dev, piece, block)
+            blocks[v] = block if h == 0 else jnp.where(place_here == h, block, blocks[v])
     for slot in range(phases):
         block = blocks[0]
         for v in range(1, variants):
@@ -374,13 +389,11 @@
 def loads_kernel(
     pan_dev,
     places,
-    kernel_scale,
     rows_ref,
     velocity_ref,
     spread_ref,
     shear_ref,
     moment_ref,
-    influence,
 ):
     owners = len(places)
     shared = LANES // pan_dev
@@ -394,47 +407,27 @@
         blocks = [rows_ref[places[q * shared + h]] for h in range(shared)]
         pieces = []
         for k in range(shared):
-            piece = None
-            for h, block in enumerate(blocks):
-                moved = block if h == k else pltpu.roll(block, (h - k) % shared * pan_dev, 1)
-                piece = moved if h == 0 else jnp.where(lane >= h * pan_dev, moved, piece)
-            pieces.append(piece)
-        panels.append(jnp.concatenate(pieces, axis=0))
-    rows = jnp.concatenate(panels, axis=1)
-    centre = rows[0:3, :]
-    area = rows[3:6, :]
-    hull = rows[6:7, :]
-    owner = rows[7:8, :]
-    weight = (
-        jnp.sqrt(
-            area[0:1, :] * area[0:1, :]
-            + area[1:2, :] * area[1:2, :]
-            + area[2:3, :] * area[2:3, :]
-            + SKIN_SQUARE
-        )
-        * kernel_scale
-    )
-    high, middle, low = in_parts(jnp.concatenate([centre, weight], axis=0))
+            piece = blocks[-k % shared]
+            for slot in range(1, shared):
+                piece = jnp.where(lane >= slot * pan_dev, blocks[(slot - k) % shared], piece)
+            pieces.append(pltpu.roll(piece, LANES - k * pan_dev, 1) if k else piece)
+        panels.append(pieces)
+
+    def tile_rows(q, begin, end):
+        if height < end - begin:
+            return jnp.concatenate(panels[q][begin // height : end // height], axis=0)
+        return panels[q][begin // height][begin % height : begin % height + end - begin, :]
+
+    centres = [tile_rows(q, 0, 4) for q in range(tiles)]
+    areas = [tile_rows(q, 4, 8) for q in range(tiles)]
+    high, middle, low = in_parts(jnp.concatenate(centres, axis=1))
     columns = dot_rows(
         jnp.concatenate([high, middle, low, jnp.zeros_like(low)], axis=0), spread_ref[...]
     )
-    blank = jnp.zeros((1, panels_total), jnp.float32)
-    area_parts = in_parts(jnp.concatenate([area, blank], axis=0))
-    velocity_parts = in_parts(
-        jnp.concatenate([velocity_ref[...], jnp.zeros((1, load_count), jnp.float32)], axis=0)
-    )
-    pairs = ((0, 0), (0, 1), (1, 0), (1, 1), (0, 2), (2, 0), (1, 2), (2, 1))
-    boundary = (
-        dot_rows(
-            jnp.concatenate([velocity_parts[k] for k, _ in pairs], axis=0),
-            jnp.concatenate([area_parts[k] for _, k in pairs], axis=0),
-        )
-        * hull
-    )
-    first = boundary.astype(jnp.bfloat16)
+    influences = {}
     for source in range(tiles):
         for target in range(source, tiles):
-            tile = panels[target]
+            tile = centres[target]
             column = columns[source * LANES : (source + 1) * LANES, :]
             column = [column[:, a * LANES : (a + 1) * LANES] for a in range(4)]
             inverse = lax.rsqrt(
@@ -443,22 +436,38 @@
                 + (tile[2:3, :] - column[2]) ** 2
                 + CORE_SQUARE
             )
-            here, there = pl.ds(source * LANES, LANES), pl.ds(target * LANES, LANES)
-            influence[here, there] = (column[3] * inverse).astype(jnp.bfloat16)
+            influences[source, target] = (column[3] * inverse).astype(jnp.bfloat16)
             if target != source:
                 other = columns[target * LANES : (target + 1) * LANES, 3 * LANES :]
-                influence[there, here] = (other * inverse.T).astype(jnp.bfloat16)
-    induced = jnp.dot(first, influence[...], preferred_element_type=jnp.float32)
+                influences[target, source] = (other * inverse.T).astype(jnp.bfloat16)
+    area_parts = in_parts(jnp.concatenate(areas, axis=1))
+    velocity_parts = in_parts(
+        jnp.concatenate([velocity_ref[...], jnp.zeros((1, load_count), jnp.float32)], axis=0)
+    )
+    pairs = ((0, 0), (0, 1), (1, 0), (1, 1), (0, 2), (2, 0), (1, 2), (2, 1))
+    boundary = dot_rows(
+        jnp.concatenate([velocity_parts[k] for k, _ in pairs], axis=0),
+        jnp.concatenate([area_parts[k] for _, k in pairs], axis=0),
+    )
+    first = boundary.astype(jnp.bfloat16)
+    influence = jnp.concatenate(
+        [
+            jnp.concatenate([influences[q, p] for p in range(tiles)], axis=1)
+            for q in range(tiles)
+        ],
+        axis=0,
+    )
+    induced = jnp.dot(first, influence, preferred_element_type=jnp.float32)
     second = (first.astype(jnp.float32) + (boundary - induced)).astype(jnp.bfloat16)
-    pressure = jnp.dot(second, influence[...], preferred_element_type=jnp.float32)
+    pressure = jnp.dot(second, influence, preferred_element_type=jnp.float32)
     stations_all = STATIONS * owners
     own_loads = jnp.zeros((load_count, LANES), jnp.float32)
     prior_loads = jnp.zeros((load_count, LANES), jnp.float32)
     prior_arms = jnp.zeros((load_count, LANES), jnp.float32)
     rank = lax.broadcasted_iota(jnp.int32, (1, LANES), 1).astype(jnp.float32)
-    for q, tile in enumerate(panels):
-        force = pressure[:, q * LANES : (q + 1) * LANES] * (tile[5:6, :] * tile[6:7, :])
-        owner = tile[7:8, :]
+    for q, tile in enumerate(areas):
+        force = pressure[:, q * LANES : (q + 1) * LANES] * tile[2:3, :]
+        owner = tile[3:4, :]
         prior = owner < 0.0
         place = (owner * STATIONS + rank) * (1.0 / stations_all)
         own_loads = own_loads + jnp.where(owner == 0.0, force, 0.0)
@@ -510,10 +519,11 @@
     control = control_points.shape[1]
     height = 8 * pan_dev // LANES
     order = [owner * phases + k for owner in range(owners)[::-1] for k in range(phases)]
+    kernel_scale = 1.0 / (4.0 * math.pi * math.sqrt(panels_total))
     vmem = pl.BlockSpec(memory_space=pltpu.VMEM)
     anywhere = pl.BlockSpec(memory_space=pl.ANY)
     rows = pl.pallas_call(
-        functools.partial(geometry_kernel, vert_dev, phases, order),
+        functools.partial(geometry_kernel, vert_dev, phases, order, kernel_scale),
         out_shape=pltpu.VMEM((members, height, LANES), jnp.float32),
         in_specs=[anywhere] * 7,
         out_specs=vmem,
@@ -541,14 +551,12 @@
         rows, ("panels", "cols", "phase"), split_axis=0, concat_axis=0, axis_index_groups=[order]
     )
     places = [order.index(owner * phases + phases - 1) for owner in range(owners)]
-    kernel_scale = 1.0 / (4.0 * math.pi * math.sqrt(panels_total))
     out = jax.ShapeDtypeStruct((1, load_count, STATIONS), jnp.float32)
     return pl.pallas_call(
-        functools.partial(loads_kernel, pan_dev, places, kernel_scale),
+        functools.partial(loads_kernel, pan_dev, places),
         out_shape=(out, out),
         in_specs=[vmem] * 3,
         out_specs=(vmem, vmem),
-        scratch_shapes=[pltpu.VMEM((panels_total, panels_total), jnp.bfloat16)],
         compiler_params=pltpu.CompilerParams(vmem_limit_bytes=32 * 1024 * 1024),
         name="loads",
     )(

time: 13.6 us -> 13.5 us (level)
  Pallas kernels: 1.81 us -> 1.66 us
    pallas_call x1, Pallas kernels: 1.74 us -> 1.59 us  [shards_whole(): pl.pallas_call(functools.partial(loads_kernel, pan_dev, places), out_shap...]
where the time goes in v7:
time: 13.5 us; the launch traced here: 13.3 us
  blocking collectives  10.9 us (81%)
  Pallas kernels  1.66 us (12%)
  between operations  0.66 us (5%)
    all_to_all x1, blocking collectives, shards_whole(): lax.all_to_all(rows, ('panels', 'cols', 'phase'), split_axis=0, concat_ax...  10.9 us
    pallas_call x1, Pallas kernels, shards_whole(): pl.pallas_call(functools.partial(loads_kernel, pan_dev, places), out_shap...  1.59 us

profile of v7, /device:TPU:0, one launch (start us, length us, event | category | flops | bytes accessed | tf_op | source)
XLA Modules:
  0.0 13.3 jit_solution(15943694755769939162)
XLA Ops:
  0.6 0.1 geometry.1
  0.7 0.0 copy-start
  0.7 0.0 copy-start.1
  0.7 10.9 %all_to_all.5.rows_ref = f32[16,4,128]{2,1,0:T(4,128)S(1)} all-to-all(f32[16,4,128]{2,1,0:T(4,128)S(1)} %geometry.1), channel_id=1, replica_groups={{14,15,12,13,10,11,8,9,6,7,4,5,2,3,0,1},{30,31,28,29,26,27,24,25,22,23,..., dimensions={0} | all-to-all | bytes 65536 | tf_op jit(solution)/shard_map/all_to_all | solution.py:550
  11.7 0.0 copy-done
  11.7 0.0 copy-done.1
  11.7 1.6 %loads.1 = (f32[1,64,128]{2,1,0:T(8,128)}, f32[1,64,128]{2,1,0:T(8,128)}) custom-call(f32[16,4,128]{2,1,0:T(4,128)S(1)} %all_to_all.5.rows_ref, f32[3,64]{1,0:T(4,128)S(1)} %bitcast.4, bf16[16,512]{1,0:T(8,128)(2,1)S(1)} %copy-done), custom_call_target="tpu_custom_call" | custom-call | tf_op jit(solution)/shard_map/loads/pallas_call | solution.py:555
Async XLA Ops:
  0.7 11.0 %copy-start = (bf16[16,512]{1,0:T(8,128)(2,1)S(1)}, bf16[16,512]{1,0:T(8,128)(2,1)}, u32[]{:S(2)}) copy-start(bf16[16,512]{1,0:T(8,128)(2,1)} %constant.2.clone.spread_ref) | copy-start | bytes 49156
  0.7 11.0 %copy-start.1 = (f32[64,3]{0,1:T(4,128)S(1)}, f32[64,3]{0,1:T(4,128)}, u32[]{:S(2)}) copy-start(f32[64,3]{0,1:T(4,128)} %param.16) | copy-start | bytes 2308

commit v8 on v7

--- a/solution.py
+++ b/solution.py
@@ -518,7 +518,8 @@
     variants = morph_weights.shape[0]
     control = control_points.shape[1]
     height = 8 * pan_dev // LANES
-    order = [owner * phases + k for owner in range(owners)[::-1] for k in range(phases)]
+    head = (owners - 1) * phases
+    order = [head] + [member for member in range(members) if member != head]
     kernel_scale = 1.0 / (4.0 * math.pi * math.sqrt(panels_total))
     vmem = pl.BlockSpec(memory_space=pltpu.VMEM)
     anywhere = pl.BlockSpec(memory_space=pl.ANY)

time: 13.5 us -> 13.3 us (0.985)
    all_to_all x1, blocking collectives: 10.9 us -> 10.8 us  [shards_whole(): lax.all_to_all(rows, ('panels', 'cols', 'phase'), split_axis=0, concat_ax...]
where the time goes in v8:
time: 13.3 us; the launch traced here: 13.1 us
  blocking collectives  10.8 us (81%)
  Pallas kernels  1.66 us (12%)
  between operations  0.66 us (5%)
    all_to_all x1, blocking collectives, shards_whole(): lax.all_to_all(rows, ('panels', 'cols', 'phase'), split_axis=0, concat_ax...  10.8 us
    pallas_call x1, Pallas kernels, shards_whole(): pl.pallas_call(functools.partial(loads_kernel, pan_dev, places), out_shap...  1.59 us

profile of v8, /device:TPU:0, one launch (start us, length us, event | category | flops | bytes accessed | tf_op | source)
XLA Modules:
  0.0 13.1 jit_solution(4864433300316962607)
XLA Ops:
  0.6 0.1 geometry.1
  0.7 0.0 copy-start
  0.7 0.0 copy-start.1
  0.7 10.8 %all_to_all.5.rows_ref = f32[16,4,128]{2,1,0:T(4,128)S(1)} all-to-all(f32[16,4,128]{2,1,0:T(4,128)S(1)} %geometry.1), channel_id=1, replica_groups={{14,0,1,2,3,4,5,6,7,8,9,10,11,12,13,15},{30,16,17,18,19,20,21,22,23,24,..., dimensions={0} | all-to-all | bytes 65536 | tf_op jit(solution)/shard_map/all_to_all | solution.py:551
  11.5 0.0 copy-done
  11.5 0.0 copy-done.1
  11.5 1.6 %loads.1 = (f32[1,64,128]{2,1,0:T(8,128)}, f32[1,64,128]{2,1,0:T(8,128)}) custom-call(f32[16,4,128]{2,1,0:T(4,128)S(1)} %all_to_all.5.rows_ref, f32[3,64]{1,0:T(4,128)S(1)} %bitcast.4, bf16[16,512]{1,0:T(8,128)(2,1)S(1)} %copy-done), custom_call_target="tpu_custom_call" | custom-call | tf_op jit(solution)/shard_map/loads/pallas_call | solution.py:556
Async XLA Ops:
  0.7 10.8 %copy-start = (bf16[16,512]{1,0:T(8,128)(2,1)S(1)}, bf16[16,512]{1,0:T(8,128)(2,1)}, u32[]{:S(2)}) copy-start(bf16[16,512]{1,0:T(8,128)(2,1)} %constant.2.clone.spread_ref) | copy-start | bytes 49156
  0.7 10.8 %copy-start.1 = (f32[64,3]{0,1:T(4,128)S(1)}, f32[64,3]{0,1:T(4,128)}, u32[]{:S(2)}) copy-start(f32[64,3]{0,1:T(4,128)} %param.16) | copy-start | bytes 2308

commit v9 on v8

--- a/solution.py
+++ b/solution.py
@@ -461,18 +461,21 @@
     second = (first.astype(jnp.float32) + (boundary - induced)).astype(jnp.bfloat16)
     pressure = jnp.dot(second, influence, preferred_element_type=jnp.float32)
     stations_all = STATIONS * owners
-    own_loads = jnp.zeros((load_count, LANES), jnp.float32)
-    prior_loads = jnp.zeros((load_count, LANES), jnp.float32)
-    prior_arms = jnp.zeros((load_count, LANES), jnp.float32)
+    inv_root = 1.0 / math.sqrt(panels_total)
     rank = lax.broadcasted_iota(jnp.int32, (1, LANES), 1).astype(jnp.float32)
+    own_loads, prior_loads, prior_arms = None, None, None
     for q, tile in enumerate(areas):
-        force = pressure[:, q * LANES : (q + 1) * LANES] * tile[2:3, :]
+        pushed = pressure[:, q * LANES : (q + 1) * LANES]
+        area = tile[2:3, :] * inv_root
         owner = tile[3:4, :]
-        prior = owner < 0.0
+        prior = jnp.where(owner < 0.0, area, 0.0)
         place = (owner * STATIONS + rank) * (1.0 / stations_all)
-        own_loads = own_loads + jnp.where(owner == 0.0, force, 0.0)
-        prior_loads = prior_loads + jnp.where(prior, force, 0.0)
-        prior_arms = prior_arms + force * jnp.where(prior, place, 0.0)
+        own_load = pushed * jnp.where(owner == 0.0, area, 0.0)
+        prior_load = pushed * prior
+        prior_arm = pushed * (prior * place)
+        own_loads = own_load if q == 0 else own_loads + own_load
+        prior_loads = prior_load if q == 0 else prior_loads + prior_load
+        prior_arms = prior_arm if q == 0 else prior_arms + prior_arm
     prior_total = jnp.sum(prior_loads, axis=1, keepdims=True)
     prior_arm = jnp.sum(prior_arms, axis=1, keepdims=True)
     station = lax.broadcasted_iota(jnp.int32, (STATIONS, 2 * STATIONS), 0)
@@ -486,16 +489,16 @@
     middle = rest.astype(jnp.bfloat16)
     low = (rest - middle.astype(jnp.float32)).astype(jnp.bfloat16)
     sums = jnp.dot(
-        jnp.concatenate([high, middle, low], axis=0), steps, preferred_element_type=jnp.float32
-    )
-    sums = sums[:load_count] + (sums[load_count : 2 * load_count] + sums[2 * load_count :])
-    inv_root = 1.0 / math.sqrt(panels_total)
-    shear_ref[0] = (prior_total + sums[:, :STATIONS]) * inv_root
+        jnp.concatenate([high, middle, low], axis=1),
+        jnp.concatenate([steps] * 3, axis=0),
+        preferred_element_type=jnp.float32,
+    )
+    shear_ref[0] = prior_total + sums[:, :STATIONS]
     moment_ref[0] = (
         (rank * (1.0 / stations_all)) * prior_total
         - prior_arm
         + sums[:, STATIONS:] * (1.0 / stations_all)
-    ) * inv_root
+    )
 
 
 def shards_whole(

time: 13.3 us -> 13.3 us (level)
  no operation moved by 1% of the time
where the time goes in v9:
time: 13.3 us; the launch traced here: 13.1 us
  blocking collectives  10.8 us (81%)
  Pallas kernels  1.65 us (12%)
  between operations  0.66 us (5%)
    all_to_all x1, blocking collectives, shards_whole(): lax.all_to_all(rows, ('panels', 'cols', 'phase'), split_axis=0, concat_ax...  10.8 us
    pallas_call x1, Pallas kernels, shards_whole(): pl.pallas_call(functools.partial(loads_kernel, pan_dev, places), out_shap...  1.57 us

profile of v9, /device:TPU:0, one launch (start us, length us, event | category | flops | bytes accessed | tf_op | source)
XLA Modules:
  0.0 13.1 jit_solution(5280347867757888404)
XLA Ops:
  0.6 0.1 geometry.1
  0.7 0.0 copy-start
  0.7 0.0 copy-start.1
  0.7 10.8 %all_to_all.5.rows_ref = f32[16,4,128]{2,1,0:T(4,128)S(1)} all-to-all(f32[16,4,128]{2,1,0:T(4,128)S(1)} %geometry.1), channel_id=1, replica_groups={{14,0,1,2,3,4,5,6,7,8,9,10,11,12,13,15},{30,16,17,18,19,20,21,22,23,24,..., dimensions={0} | all-to-all | bytes 65536 | tf_op jit(solution)/shard_map/all_to_all | solution.py:554
  11.5 0.0 copy-done
  11.5 0.0 copy-done.1
  11.5 1.6 %loads.1 = (f32[1,64,128]{2,1,0:T(8,128)}, f32[1,64,128]{2,1,0:T(8,128)}) custom-call(f32[16,4,128]{2,1,0:T(4,128)S(1)} %all_to_all.5.rows_ref, f32[3,64]{1,0:T(4,128)S(1)} %bitcast.4, bf16[16,512]{1,0:T(8,128)(2,1)S(1)} %copy-done), custom_call_target="tpu_custom_call" | custom-call | tf_op jit(solution)/shard_map/loads/pallas_call | solution.py:559
Async XLA Ops:
  0.7 10.8 %copy-start = (bf16[16,512]{1,0:T(8,128)(2,1)S(1)}, bf16[16,512]{1,0:T(8,128)(2,1)}, u32[]{:S(2)}) copy-start(bf16[16,512]{1,0:T(8,128)(2,1)} %constant.2.clone.spread_ref) | copy-start | bytes 49156
  0.7 10.8 %copy-start.1 = (f32[64,3]{0,1:T(4,128)S(1)}, f32[64,3]{0,1:T(4,128)}, u32[]{:S(2)}) copy-start(f32[64,3]{0,1:T(4,128)} %param.16) | copy-start | bytes 2308

commit v10 on v9

--- a/solution.py
+++ b/solution.py
@@ -425,8 +425,8 @@
         jnp.concatenate([high, middle, low, jnp.zeros_like(low)], axis=0), spread_ref[...]
     )
     influences = {}
-    for source in range(tiles):
-        for target in range(source, tiles):
+    for target in range(tiles):
+        for source in range(target + 1):
             tile = centres[target]
             column = columns[source * LANES : (source + 1) * LANES, :]
             column = [column[:, a * LANES : (a + 1) * LANES] for a in range(4)]

time: 13.3 us -> 13.3 us (level)
  no operation moved by 1% of the time
where the time goes in v10:
time: 13.3 us; the launch traced here: 13.1 us
  blocking collectives  10.8 us (81%)
  Pallas kernels  1.65 us (12%)
  between operations  0.66 us (5%)
    all_to_all x1, blocking collectives, shards_whole(): lax.all_to_all(rows, ('panels', 'cols', 'phase'), split_axis=0, concat_ax...  10.8 us
    pallas_call x1, Pallas kernels, shards_whole(): pl.pallas_call(functools.partial(loads_kernel, pan_dev, places), out_shap...  1.57 us

profile of v10, /device:TPU:0, one launch (start us, length us, event | category | flops | bytes accessed | tf_op | source)
XLA Modules:
  0.0 13.1 jit_solution(5280347867757888404)
XLA Ops:
  0.6 0.1 geometry.1
  0.7 0.0 copy-start
  0.7 0.0 copy-start.1
  0.7 10.8 %all_to_all.5.rows_ref = f32[16,4,128]{2,1,0:T(4,128)S(1)} all-to-all(f32[16,4,128]{2,1,0:T(4,128)S(1)} %geometry.1), channel_id=1, replica_groups={{14,0,1,2,3,4,5,6,7,8,9,10,11,12,13,15},{30,16,17,18,19,20,21,22,23,24,..., dimensions={0} | all-to-all | bytes 65536 | tf_op jit(solution)/shard_map/all_to_all | solution.py:554
  11.5 0.0 copy-done
  11.5 0.0 copy-done.1
  11.5 1.6 %loads.1 = (f32[1,64,128]{2,1,0:T(8,128)}, f32[1,64,128]{2,1,0:T(8,128)}) custom-call(f32[16,4,128]{2,1,0:T(4,128)S(1)} %all_to_all.5.rows_ref, f32[3,64]{1,0:T(4,128)S(1)} %bitcast.4, bf16[16,512]{1,0:T(8,128)(2,1)S(1)} %copy-done), custom_call_target="tpu_custom_call" | custom-call | tf_op jit(solution)/shard_map/loads/pallas_call | solution.py:559
Async XLA Ops:
  0.7 10.8 %copy-start = (bf16[16,512]{1,0:T(8,128)(2,1)S(1)}, bf16[16,512]{1,0:T(8,128)(2,1)}, u32[]{:S(2)}) copy-start(bf16[16,512]{1,0:T(8,128)(2,1)} %constant.2.clone.spread_ref) | copy-start | bytes 49156
  0.7 10.8 %copy-start.1 = (f32[64,3]{0,1:T(4,128)S(1)}, f32[64,3]{0,1:T(4,128)}, u32[]{:S(2)}) copy-start(f32[64,3]{0,1:T(4,128)} %param.16) | copy-start | bytes 2308
